TPU v7x, 128 devices: a whole 4x4x4 slice. The times are simulated.
128 devices in a mesh: dp: 8 (over y, x_hi), graph: 16 (over x_lo, z, core).
Axes of the slice: x: 4 (x_hi: 2, x_lo: 2; x = x_hi * 2 + x_lo), y: 4, z: 4, core: 2. Of those that a mesh axis runs over, the one named last changes fastest.
Arguments:
- node_state: bfloat16 [8, 14336, 128], P('dp', 'graph'), may hold values from -6 to 6
- atom_types: int32 [8, 14336], P('dp', 'graph'), may hold values from 0 to 89
- positions: float32 [8, 3, 14336], P('dp', None, 'graph'), may hold values from 0 to 6
- force_ref: float32 [8, 3, 14336], P('dp', None, 'graph'), may hold values from -8 to 8
- edge_source: int32 [8, 286720], P('dp', 'graph'), may hold values from 0 to 14335, as said below
- edge_count: int32 [8, 16], P('dp', 'graph'), may hold values from 8960 to 17920, as said below
- type_table: bfloat16 [90, 128], replicated, may hold values from -3 to 3
- w_rad: bfloat16 [256, 128], replicated, may hold values from -3 to 3
- w_src: bfloat16 [128, 128], replicated, may hold values from -0.5 to 0.5
- w_out: float32 [128], replicated, may hold values from -0.06 to 0.06
Outputs:
- forces: float32 [8, 3, 14336], P('dp', None, 'graph')
- grad_radial: float32 [256, 128], replicated
- grad_source: float32 [128, 128], replicated
- grad_out: float32 [128], replicated
- loss: float32 [], replicated
Inputs may be any that keep to these rules, and one draw needn't show every extreme that they name: `edge_source`: of the slots of block k (slots k*17920 to (k+1)*17920 - 1), the first 2240 name a source node of the block half the number of blocks away from k, taken around; every other slot names a source node of block k-1, k or k+1, taken around the ends, and never its own target node (slot e // 20); blocks hold 896 nodes each. `edge_count`: in every batch some block has all 17920 slots live.
All inputs are finite; a program needn't handle non-finite values.
Results may differ from a plain program's by a relative error of at most 0.0049.
Values may be sent and summed in bfloat16 or wider, within the bound.
A program may use at most 192 MiB of HBM per device.

v0:
```python
import math

import jax
import jax.numpy as jnp
from jax import lax
from jax.sharding import PartitionSpec as P


def basis(dist, count):
    centers = jnp.arange(count, dtype=jnp.float32) * (12.0 / count)
    gamma = count * count / 1152.0
    diff = dist[:, None] - centers[None, :]
    bump = jnp.exp(-gamma * diff * diff)
    return (bump.astype(jnp.bfloat16), (-2.0 * gamma * diff * bump).astype(jnp.bfloat16))


def derivatives(agg):
    sig = jax.nn.sigmoid(agg)
    first = sig * (1.0 + agg * (1.0 - sig))
    second = sig * (1.0 - sig) * (2.0 + agg * (1.0 - 2.0 * sig))
    return (first, second)


def block_number(slots):
    pieces = max(1, -(-slots // 2048))
    while slots % pieces != 0:
        pieces = pieces + 1
    return pieces


def select_matrix(picked_block, table_rows):
    return (picked_block[:, None] == jnp.arange(table_rows, dtype=jnp.int32)[None, :]).astype(
        jnp.float32
    )


def pick_columns(table, picked, pieces):
    table_rows = table.shape[1]
    blocks = picked.reshape(pieces, -1)

    def one_block(picked_block):
        select = select_matrix(picked_block, table_rows)
        return lax.dot_general(
            table,
            select,
            (((1,), (1,)), ((), ())),
            precision=lax.Precision.HIGHEST,
            preferred_element_type=jnp.float32,
        )

    result = lax.map(one_block, blocks)
    return jnp.transpose(result, (1, 0, 2)).reshape(table.shape[0], -1)


def spread_columns(values, picked, table_rows, pieces):
    blocks = picked.reshape(pieces, -1)
    value_blocks = jnp.transpose(values.reshape(values.shape[0], pieces, -1), (1, 0, 2))

    def add_block(total, items):
        picked_block, value_block = items
        select = select_matrix(picked_block, table_rows)
        return (
            total
            + jnp.dot(
                value_block,
                select,
                precision=lax.Precision.HIGHEST,
                preferred_element_type=jnp.float32,
            ),
            None,
        )

    start_total = jnp.zeros((values.shape[0], table_rows), jnp.float32)
    total, unused = lax.scan(add_block, start_total, (blocks, value_blocks))
    return total


def widen(values, nodes, degree):
    return jnp.broadcast_to(values[:, :, None], (values.shape[0], nodes, degree)).reshape(
        values.shape[0], nodes * degree
    )


def widen_rows(values, nodes, degree):
    return jnp.broadcast_to(values[:, None, :], (nodes, degree, values.shape[1])).reshape(
        nodes * degree, values.shape[1]
    )


def four_blocks(whole, index, groups, nodes, axis, offsets):
    pieces_list = [
        lax.dynamic_slice_in_dim(whole, (index + shift_by + groups) % groups * nodes, nodes, axis)
        for shift_by in offsets
    ]
    return jnp.concatenate(pieces_list, axis=axis)


def local(
    node_state,
    atom_types,
    positions,
    force_ref,
    edge_source,
    edge_count,
    type_table,
    w_rad,
    w_src,
    w_out,
):
    nodes = node_state.shape[1]
    groups = lax.axis_size("graph")
    half_way = groups // 2
    index = lax.axis_index("graph")
    weight_loss = 1.0 / math.sqrt(3.0 * nodes * groups * node_state.shape[0] * lax.axis_size("dp"))
    kinds = type_table.shape[0]
    basis_count = w_rad.shape[0]
    channels = node_state.shape[2]
    onehot = (atom_types[0][:, None] == jnp.arange(kinds, dtype=jnp.int32)[None, :]).astype(
        jnp.bfloat16
    )
    embedded = jnp.dot(onehot, type_table, preferred_element_type=jnp.float32)
    state = (node_state[0].astype(jnp.float32) + embedded).astype(jnp.bfloat16)
    places = positions[0]
    source = edge_source[0]
    slots = source.shape[0]
    degree = slots // nodes
    pieces = block_number(slots)
    live = (jnp.arange(slots, dtype=jnp.int32) < edge_count[0, 0]).astype(jnp.float32)
    offsets = (-1, 0, 1, half_way)
    offset = (source // nodes - index + groups) % groups
    position = jnp.where(
        offset == groups - 1, 0, jnp.where(offset == 0, 1, jnp.where(offset == 1, 2, 3))
    )
    picked = position * nodes + source % nodes
    table_rows = 4 * nodes
    gathered_state = lax.all_gather(state, "graph", axis=0, tiled=True)
    gathered_place = lax.all_gather(places, "graph", axis=1, tiled=True)
    every_state = four_blocks(gathered_state, index, groups, nodes, 0, offsets)
    every_place = four_blocks(gathered_place, index, groups, nodes, 1, offsets)
    source_rows = jnp.take(every_state, picked, axis=0)
    delta = pick_columns(every_place, picked, pieces) - widen(places, nodes, degree)
    dist = jnp.sqrt(jnp.sum(delta * delta, axis=0) + 0.25)
    unit = delta / dist
    rbf, drbf = basis(dist, basis_count)
    radial = jnp.dot(rbf, w_rad, preferred_element_type=jnp.float32)
    slope = jnp.dot(drbf, w_rad, preferred_element_type=jnp.float32)
    query = jnp.dot(source_rows, w_src, preferred_element_type=jnp.float32)
    agg = 0.2 * jnp.sum((live[:, None] * radial * query).reshape(nodes, degree, channels), axis=1)
    first, second = derivatives(agg)
    readout = first * w_out
    readout_edges = widen_rows(readout, nodes, degree)
    pull = 0.2 * live * jnp.sum(readout_edges * query * slope, axis=1)
    moved = pull[None, :] * unit
    incoming = jnp.sum(moved.reshape(3, nodes, degree), axis=2)
    outgoing = spread_columns(moved, picked, table_rows, pieces)
    spread = jnp.zeros((3, groups * nodes), jnp.float32)
    for slot_index in range(4):
        block_start = (index + offsets[slot_index] + groups) % groups * nodes
        spread = lax.dynamic_update_slice_in_dim(
            spread, outgoing[:, slot_index * nodes : (slot_index + 1) * nodes], block_start, 1
        )
    leaving = lax.psum_scatter(spread, "graph", scatter_dimension=1, tiled=True)
    forces = incoming - leaving
    miss = forces - force_ref[0]
    loss_part = weight_loss * jnp.sum(miss * miss)
    back = 2.0 * weight_loss * miss
    gathered_back = lax.all_gather(back, "graph", axis=1, tiled=True)
    every_back = four_blocks(gathered_back, index, groups, nodes, 1, offsets)
    lam = live * jnp.sum(
        (widen(back, nodes, degree) - pick_columns(every_back, picked, pieces)) * unit, axis=0
    )
    over_slope = 0.2 * lam[:, None] * readout_edges
    dread = 0.2 * jnp.sum((lam[:, None] * query * slope).reshape(nodes, degree, channels), axis=1)
    grad_out_part = jnp.sum(dread * first, axis=0)
    over_plain = 0.2 * live[:, None] * widen_rows(dread * w_out * second, nodes, degree)
    coef_plain = (over_plain * query).astype(jnp.bfloat16)
    coef_slope = (over_slope * query).astype(jnp.bfloat16)
    dquery = (over_slope * slope + over_plain * radial).astype(jnp.bfloat16)
    grad_radial_part = jnp.dot(rbf.T, coef_plain, preferred_element_type=jnp.float32) + jnp.dot(
        drbf.T, coef_slope, preferred_element_type=jnp.float32
    )
    grad_source_part = jnp.dot(source_rows.T, dquery, preferred_element_type=jnp.float32)
    stacked = jnp.concatenate([grad_radial_part, grad_source_part], axis=0)
    stacked, grad_out, loss = lax.psum((stacked, grad_out_part, loss_part), ("dp", "graph"))
    return (forces[None], stacked[:basis_count], stacked[basis_count:], grad_out, loss)


def solution(mesh):
    in_specs = (
        P("dp", "graph", None),
        P("dp", "graph"),
        P("dp", None, "graph"),
        P("dp", None, "graph"),
        P("dp", "graph"),
        P("dp", "graph"),
        P(),
        P(),
        P(),
        P(),
    )
    out_specs = (P("dp", None, "graph"), P(), P(), P(), P())
    return jax.shard_map(local, mesh=mesh, in_specs=in_specs, out_specs=out_specs, check_vma=False)
```

profile of v0, /device:TPU:1, one launch (start us, length us, event | category | flops | bytes accessed | tf_op | source)
XLA Modules:
  0.0 883.5 jit_solution(5744086198159644471)
XLA Ops:
  7.9 2.0 fusion.25
  10.0 1.3 remainder_reduce_fusion
  12.4 2.1 fusion.49
  14.6 23.1 %all-gather = f32[1,3,14336]{2,0,1:T(1,128)S(1)} all-gather(f32[1,3,896]{2,0,1:T(1,128)} %param.18), channel_id=2, replica_groups=mesh['dp'=8,'graph'=16] {'graph'}, dimensions={2}, use_global_device_ids=true | all-gather | bytes 182784 | tf_op jit(solution)/shard_map/all_gather | solution.py:137
  40.6 118.5 %while.31 = (s32[]{:T(128)}, f32[10,3,1792]{2,0,1:T(8,128)S(1)}, s32[10,1792]{1,0:T(8,128)S(1)}, f32[3,3584]{1,0:T(4,128)S(1)}, s32[]{:T(128)}, /*index=5*/s32[]{:T(128)}) while((s32[]{:T(128)}, f32[10,3,1792]{2,0,1:T(8,128)S(1)}, s32[10,1792]{1,0:T(8,128)S(1)}, f32[3,3584]{1,0:T(4,128)S(1)}, s32[]{:T(128)}, /*index=5*/s32[]{:T(128)}) %tuple.73), condition=%wide.region_1.2_spmd, body=%wide.region_0.1_spmd.sunk | while | flops 237633536 | bytes 172117 | solution.py:51
  40.9 11.5 %fusion.73 = f32[1,3,1792]{2,1,0:T(4,128)S(1)} fusion(f32[3,3584]{1,0:T(4,128)S(1)} %get-tuple-element.247, s32[1792]{0:T(1024)S(1)} %dynamic-slice_reduce_fusion.6), kind=kOutput, calls=%fused_computation.4.clone.1 | convolution fusion | flops 237633536 | bytes 71680 | tf_op jit(solution)/shard_map/while/body/eval_jaxpr/dot_general | solution.py:43
  52.7 11.5 %fusion.73 = f32[1,3,1792]{2,1,0:T(4,128)S(1)} fusion(f32[3,3584]{1,0:T(4,128)S(1)} %get-tuple-element.247, s32[1792]{0:T(1024)S(1)} %dynamic-slice_reduce_fusion.6), kind=kOutput, calls=%fused_computation.4.clone.1 | convolution fusion | flops 237633536 | bytes 71680 | tf_op jit(solution)/shard_map/while/body/eval_jaxpr/dot_general | solution.py:43
  64.5 11.5 %fusion.73 = f32[1,3,1792]{2,1,0:T(4,128)S(1)} fusion(f32[3,3584]{1,0:T(4,128)S(1)} %get-tuple-element.247, s32[1792]{0:T(1024)S(1)} %dynamic-slice_reduce_fusion.6), kind=kOutput, calls=%fused_computation.4.clone.1 | convolution fusion | flops 237633536 | bytes 71680 | tf_op jit(solution)/shard_map/while/body/eval_jaxpr/dot_general | solution.py:43
  76.4 11.5 %fusion.73 = f32[1,3,1792]{2,1,0:T(4,128)S(1)} fusion(f32[3,3584]{1,0:T(4,128)S(1)} %get-tuple-element.247, s32[1792]{0:T(1024)S(1)} %dynamic-slice_reduce_fusion.6), kind=kOutput, calls=%fused_computation.4.clone.1 | convolution fusion | flops 237633536 | bytes 71680 | tf_op jit(solution)/shard_map/while/body/eval_jaxpr/dot_general | solution.py:43
  88.2 11.5 %fusion.73 = f32[1,3,1792]{2,1,0:T(4,128)S(1)} fusion(f32[3,3584]{1,0:T(4,128)S(1)} %get-tuple-element.247, s32[1792]{0:T(1024)S(1)} %dynamic-slice_reduce_fusion.6), kind=kOutput, calls=%fused_computation.4.clone.1 | convolution fusion | flops 237633536 | bytes 71680 | tf_op jit(solution)/shard_map/while/body/eval_jaxpr/dot_general | solution.py:43
  100.0 11.5 %fusion.73 = f32[1,3,1792]{2,1,0:T(4,128)S(1)} fusion(f32[3,3584]{1,0:T(4,128)S(1)} %get-tuple-element.247, s32[1792]{0:T(1024)S(1)} %dynamic-slice_reduce_fusion.6), kind=kOutput, calls=%fused_computation.4.clone.1 | convolution fusion | flops 237633536 | bytes 71680 | tf_op jit(solution)/shard_map/while/body/eval_jaxpr/dot_general | solution.py:43
  111.9 11.5 %fusion.73 = f32[1,3,1792]{2,1,0:T(4,128)S(1)} fusion(f32[3,3584]{1,0:T(4,128)S(1)} %get-tuple-element.247, s32[1792]{0:T(1024)S(1)} %dynamic-slice_reduce_fusion.6), kind=kOutput, calls=%fused_computation.4.clone.1 | convolution fusion | flops 237633536 | bytes 71680 | tf_op jit(solution)/shard_map/while/body/eval_jaxpr/dot_general | solution.py:43
  123.7 11.5 %fusion.73 = f32[1,3,1792]{2,1,0:T(4,128)S(1)} fusion(f32[3,3584]{1,0:T(4,128)S(1)} %get-tuple-element.247, s32[1792]{0:T(1024)S(1)} %dynamic-slice_reduce_fusion.6), kind=kOutput, calls=%fused_computation.4.clone.1 | convolution fusion | flops 237633536 | bytes 71680 | tf_op jit(solution)/shard_map/while/body/eval_jaxpr/dot_general | solution.py:43
  135.5 11.5 %fusion.73 = f32[1,3,1792]{2,1,0:T(4,128)S(1)} fusion(f32[3,3584]{1,0:T(4,128)S(1)} %get-tuple-element.247, s32[1792]{0:T(1024)S(1)} %dynamic-slice_reduce_fusion.6), kind=kOutput, calls=%fused_computation.4.clone.1 | convolution fusion | flops 237633536 | bytes 71680 | tf_op jit(solution)/shard_map/while/body/eval_jaxpr/dot_general | solution.py:43
  147.4 11.5 %fusion.73 = f32[1,3,1792]{2,1,0:T(4,128)S(1)} fusion(f32[3,3584]{1,0:T(4,128)S(1)} %get-tuple-element.247, s32[1792]{0:T(1024)S(1)} %dynamic-slice_reduce_fusion.6), kind=kOutput, calls=%fused_computation.4.clone.1 | convolution fusion | flops 237633536 | bytes 71680 | tf_op jit(solution)/shard_map/while/body/eval_jaxpr/dot_general | solution.py:43
  159.9 1.3 sqrt.21
  161.2 1.6 reshape.346
  164.4 9.8 %fusion.19 = f32[17920,128]{1,0:T(8,128)} fusion(bf16[256,128]{1,0:T(8,128)(2,1)S(1)} %copy-done, f32[256]{0:T(256)S(1)} %iota_multiply_fusion, f32[17920]{0:T(1024)S(1)} %sqrt.20), kind=kOutput, calls=%fused_computation.34 | convolution fusion | flops 1192755200 | bytes 9313280 | tf_op jit(solution)/shard_map/dot_general | solution.py:145
  174.2 1.3 constant_dynamic-slice_fusion.8
  175.6 36.7 %gather_fusion = bf16[17920,128]{1,0:T(8,128)(2,1)} fusion(bf16[3584,128]{1,0:T(8,128)(2,1)S(1)} %pad_maximum_fusion, s32[18432]{0:T(1024)S(1)} %copy-done.4), kind=kCustom, calls=%fused_computation | custom fusion | bytes 9246720 | tf_op jit(solution)/shard_map/jit(_take)/gather | solution.py:140
  212.3 17.8 %multiply_multiply_fusion.1 = (f32[17920,128]{1,0:T(8,128)}, f32[17920,128]{1,0:T(8,128)}) fusion(f32[17920,128]{1,0:T(8,128)} %fusion.19, f32[17920]{0:T(1024)S(1)} %fusion.47, bf16[128,128]{1,0:T(8,128)(2,1)S(1)} %copy-done.8, bf16[17920,128]{1,0:T(8,128)(2,1)} %gather_fusion, pred[17920]{0:T(1024)(128)(4,1)S(1)} %compare_and_fusion), kind=kOutput, calls=%fused_computation.30 | convolution fusion | flops 594083840 | bytes 32235008 | tf_op jit(solution)/shard_map/dot_general | solution.py:147
  230.1 10.8 %reshape.344 = f32[896,20,128]{2,1,0:T(8,128)} reshape(f32[17920,128]{1,0:T(8,128)} %get-tuple-element.149) | data formatting | bytes 18350080 | tf_op jit(solution)/shard_map/reshape | solution.py:148
  240.8 6.0 reduce_sum.79
  247.0 4.9 broadcast_in_dim.96
  251.9 11.0 %reshape.345 = f32[17920,128]{1,0:T(8,128)} reshape(f32[896,20,128]{2,1,0:T(8,128)} %broadcast_in_dim.96) | data formatting | bytes 18350080 | tf_op jit(solution)/shard_map/reshape | solution.py:85
  262.9 13.8 %multiply_reduce_fusion = (f32[17920]{0:T(1024)S(1)}, f32[17920,128]{1,0:T(8,128)}) fusion(f32[17920,128]{1,0:T(8,128)} %reshape.345, f32[17920,128]{1,0:T(8,128)} %get-tuple-element.150, bf16[256,128]{1,0:T(8,128)(2,1)S(1)} %copy-done, f32[256]{0:T(256)S(1)} %iota_multiply_fusion, f32[17920]{0:T(1024)S(1)} %copy-done.6), kind=kOutput, calls=%fused_computation.29 | convolution fusion | flops 1208793600 | bytes 27735040 | tf_op jit(solution)/shard_map/dot_general | solution.py:146
  278.1 113.2 %while.33 = (s32[]{:T(128)}, f32[3,3584]{1,0:T(4,128)}, f32[10,3,1792]{2,0,1:T(8,128)}, s32[10,1792]{1,0:T(8,128)}, s32[]{:T(128)}, /*index=5*/s32[]{:T(128)}) while((s32[]{:T(128)}, f32[3,3584]{1,0:T(4,128)}, f32[10,3,1792]{2,0,1:T(8,128)}, s32[10,1792]{1,0:T(8,128)}, s32[]{:T(128)}, /*index=5*/s32[]{:T(128)}) %tuple.88), condition=%wide.region_7.8_spmd.clone, body=%wide.region_6.7_spmd.clone.sunk | while | flops 237655040 | bytes 172127 | solution.py:74
  280.2 8.8 fusion.76
  290.8 9.6 %fusion.76 = f32[3,3584]{1,0:T(4,128)} fusion(s32[1792]{0:T(1024)S(1)} %dynamic-slice_reduce_fusion.8, f32[3,3584]{1,0:T(4,128)} %get-tuple-element.257, f32[1,3,1792]{2,0,1:T(1,128)S(1)} %constant_dynamic-slice_fusion.14, pred[]{:T(512)S(6)} %compare.16), kind=kOutput, calls=%fused_computation.14.clone.1 | convolution fusion | flops 237655040 | bytes 114689 | tf_op jit(solution)/shard_map/while/body/eval_jaxpr/dot_general | solution.py:64
  302.2 9.6 %fusion.76 = f32[3,3584]{1,0:T(4,128)} fusion(s32[1792]{0:T(1024)S(1)} %dynamic-slice_reduce_fusion.8, f32[3,3584]{1,0:T(4,128)} %get-tuple-element.257, f32[1,3,1792]{2,0,1:T(1,128)S(1)} %constant_dynamic-slice_fusion.14, pred[]{:T(512)S(6)} %compare.16), kind=kOutput, calls=%fused_computation.14.clone.1 | convolution fusion | flops 237655040 | bytes 114689 | tf_op jit(solution)/shard_map/while/body/eval_jaxpr/dot_general | solution.py:64
  313.5 9.6 %fusion.76 = f32[3,3584]{1,0:T(4,128)} fusion(s32[1792]{0:T(1024)S(1)} %dynamic-slice_reduce_fusion.8, f32[3,3584]{1,0:T(4,128)} %get-tuple-element.257, f32[1,3,1792]{2,0,1:T(1,128)S(1)} %constant_dynamic-slice_fusion.14, pred[]{:T(512)S(6)} %compare.16), kind=kOutput, calls=%fused_computation.14.clone.1 | convolution fusion | flops 237655040 | bytes 114689 | tf_op jit(solution)/shard_map/while/body/eval_jaxpr/dot_general | solution.py:64
  324.9 9.6 %fusion.76 = f32[3,3584]{1,0:T(4,128)} fusion(s32[1792]{0:T(1024)S(1)} %dynamic-slice_reduce_fusion.8, f32[3,3584]{1,0:T(4,128)} %get-tuple-element.257, f32[1,3,1792]{2,0,1:T(1,128)S(1)} %constant_dynamic-slice_fusion.14, pred[]{:T(512)S(6)} %compare.16), kind=kOutput, calls=%fused_computation.14.clone.1 | convolution fusion | flops 237655040 | bytes 114689 | tf_op jit(solution)/shard_map/while/body/eval_jaxpr/dot_general | solution.py:64
  336.3 9.6 %fusion.76 = f32[3,3584]{1,0:T(4,128)} fusion(s32[1792]{0:T(1024)S(1)} %dynamic-slice_reduce_fusion.8, f32[3,3584]{1,0:T(4,128)} %get-tuple-element.257, f32[1,3,1792]{2,0,1:T(1,128)S(1)} %constant_dynamic-slice_fusion.14, pred[]{:T(512)S(6)} %compare.16), kind=kOutput, calls=%fused_computation.14.clone.1 | convolution fusion | flops 237655040 | bytes 114689 | tf_op jit(solution)/shard_map/while/body/eval_jaxpr/dot_general | solution.py:64
  347.6 9.6 %fusion.76 = f32[3,3584]{1,0:T(4,128)} fusion(s32[1792]{0:T(1024)S(1)} %dynamic-slice_reduce_fusion.8, f32[3,3584]{1,0:T(4,128)} %get-tuple-element.257, f32[1,3,1792]{2,0,1:T(1,128)S(1)} %constant_dynamic-slice_fusion.14, pred[]{:T(512)S(6)} %compare.16), kind=kOutput, calls=%fused_computation.14.clone.1 | convolution fusion | flops 237655040 | bytes 114689 | tf_op jit(solution)/shard_map/while/body/eval_jaxpr/dot_general | solution.py:64
  359.0 9.6 %fusion.76 = f32[3,3584]{1,0:T(4,128)} fusion(s32[1792]{0:T(1024)S(1)} %dynamic-slice_reduce_fusion.8, f32[3,3584]{1,0:T(4,128)} %get-tuple-element.257, f32[1,3,1792]{2,0,1:T(1,128)S(1)} %constant_dynamic-slice_fusion.14, pred[]{:T(512)S(6)} %compare.16), kind=kOutput, calls=%fused_computation.14.clone.1 | convolution fusion | flops 237655040 | bytes 114689 | tf_op jit(solution)/shard_map/while/body/eval_jaxpr/dot_general | solution.py:64
  370.4 9.6 %fusion.76 = f32[3,3584]{1,0:T(4,128)} fusion(s32[1792]{0:T(1024)S(1)} %dynamic-slice_reduce_fusion.8, f32[3,3584]{1,0:T(4,128)} %get-tuple-element.257, f32[1,3,1792]{2,0,1:T(1,128)S(1)} %constant_dynamic-slice_fusion.14, pred[]{:T(512)S(6)} %compare.16), kind=kOutput, calls=%fused_computation.14.clone.1 | convolution fusion | flops 237655040 | bytes 114689 | tf_op jit(solution)/shard_map/while/body/eval_jaxpr/dot_general | solution.py:64
  381.7 9.6 %fusion.76 = f32[3,3584]{1,0:T(4,128)} fusion(s32[1792]{0:T(1024)S(1)} %dynamic-slice_reduce_fusion.8, f32[3,3584]{1,0:T(4,128)} %get-tuple-element.257, f32[1,3,1792]{2,0,1:T(1,128)S(1)} %constant_dynamic-slice_fusion.14, pred[]{:T(512)S(6)} %compare.16), kind=kOutput, calls=%fused_computation.14.clone.1 | convolution fusion | flops 237655040 | bytes 114689 | tf_op jit(solution)/shard_map/while/body/eval_jaxpr/dot_general | solution.py:64
  394.2 4.6 copy.22
  399.0 1.9 multiply_reduce_fusion.1
  400.9 65.3 %reduce-scatter.4.cloned.1.call-done = f32[896,3]{1,0:T(8,128)} async-done(((f32[14336,3]{1,0:T(8,128)}), f32[896,3]{1,0:T(8,128)}) %reduce-scatter.4.cloned.1.call-update) | async-done | bytes 10768
  468.0 21.1 %all_gather.11 = f32[3,14336]{1,0:T(4,128)S(1)} all-gather(f32[3,896]{1,0:T(4,128)S(1)} %get-tuple-element.147), channel_id=1, replica_groups=mesh['dp'=8,'graph'=16] {'graph'}, dimensions={1}, use_global_device_ids=true | all-gather | bytes 182784 | tf_op jit(solution)/shard_map/all_gather | solution.py:167
  490.8 126.6 %while.32 = (s32[]{:T(128)}, f32[10,3,1792]{2,0,1:T(8,128)S(1)}, s32[10,1792]{1,0:T(8,128)}, f32[3,3584]{1,0:T(4,128)S(1)}, s32[]{:T(128)}, /*index=5*/s32[]{:T(128)}) while((s32[]{:T(128)}, f32[10,3,1792]{2,0,1:T(8,128)S(1)}, s32[10,1792]{1,0:T(8,128)}, f32[3,3584]{1,0:T(4,128)S(1)}, s32[]{:T(128)}, /*index=5*/s32[]{:T(128)}) %tuple.89), condition=%wide.region_10.11_spmd, body=%wide.region_9.10_spmd.sunk | while | flops 237633536 | bytes 172117 | solution.py:51
  491.9 11.5 %fusion.75 = f32[1,3,1792]{2,1,0:T(4,128)S(1)} fusion(f32[3,3584]{1,0:T(4,128)S(1)} %get-tuple-element.283, s32[1792]{0:T(1024)S(1)} %dynamic-slice_reduce_fusion.7), kind=kOutput, calls=%fused_computation.9.clone.1 | convolution fusion | flops 237633536 | bytes 71680 | tf_op jit(solution)/shard_map/while/body/eval_jaxpr/dot_general | solution.py:43
  504.5 11.5 %fusion.75 = f32[1,3,1792]{2,1,0:T(4,128)S(1)} fusion(f32[3,3584]{1,0:T(4,128)S(1)} %get-tuple-element.283, s32[1792]{0:T(1024)S(1)} %dynamic-slice_reduce_fusion.7), kind=kOutput, calls=%fused_computation.9.clone.1 | convolution fusion | flops 237633536 | bytes 71680 | tf_op jit(solution)/shard_map/while/body/eval_jaxpr/dot_general | solution.py:43
  517.1 11.5 %fusion.75 = f32[1,3,1792]{2,1,0:T(4,128)S(1)} fusion(f32[3,3584]{1,0:T(4,128)S(1)} %get-tuple-element.283, s32[1792]{0:T(1024)S(1)} %dynamic-slice_reduce_fusion.7), kind=kOutput, calls=%fused_computation.9.clone.1 | convolution fusion | flops 237633536 | bytes 71680 | tf_op jit(solution)/shard_map/while/body/eval_jaxpr/dot_general | solution.py:43
  529.8 11.5 %fusion.75 = f32[1,3,1792]{2,1,0:T(4,128)S(1)} fusion(f32[3,3584]{1,0:T(4,128)S(1)} %get-tuple-element.283, s32[1792]{0:T(1024)S(1)} %dynamic-slice_reduce_fusion.7), kind=kOutput, calls=%fused_computation.9.clone.1 | convolution fusion | flops 237633536 | bytes 71680 | tf_op jit(solution)/shard_map/while/body/eval_jaxpr/dot_general | solution.py:43
  542.4 11.5 %fusion.75 = f32[1,3,1792]{2,1,0:T(4,128)S(1)} fusion(f32[3,3584]{1,0:T(4,128)S(1)} %get-tuple-element.283, s32[1792]{0:T(1024)S(1)} %dynamic-slice_reduce_fusion.7), kind=kOutput, calls=%fused_computation.9.clone.1 | convolution fusion | flops 237633536 | bytes 71680 | tf_op jit(solution)/shard_map/while/body/eval_jaxpr/dot_general | solution.py:43
  555.1 11.5 %fusion.75 = f32[1,3,1792]{2,1,0:T(4,128)S(1)} fusion(f32[3,3584]{1,0:T(4,128)S(1)} %get-tuple-element.283, s32[1792]{0:T(1024)S(1)} %dynamic-slice_reduce_fusion.7), kind=kOutput, calls=%fused_computation.9.clone.1 | convolution fusion | flops 237633536 | bytes 71680 | tf_op jit(solution)/shard_map/while/body/eval_jaxpr/dot_general | solution.py:43
  567.7 11.5 %fusion.75 = f32[1,3,1792]{2,1,0:T(4,128)S(1)} fusion(f32[3,3584]{1,0:T(4,128)S(1)} %get-tuple-element.283, s32[1792]{0:T(1024)S(1)} %dynamic-slice_reduce_fusion.7), kind=kOutput, calls=%fused_computation.9.clone.1 | convolution fusion | flops 237633536 | bytes 71680 | tf_op jit(solution)/shard_map/while/body/eval_jaxpr/dot_general | solution.py:43
  580.4 11.5 %fusion.75 = f32[1,3,1792]{2,1,0:T(4,128)S(1)} fusion(f32[3,3584]{1,0:T(4,128)S(1)} %get-tuple-element.283, s32[1792]{0:T(1024)S(1)} %dynamic-slice_reduce_fusion.7), kind=kOutput, calls=%fused_computation.9.clone.1 | convolution fusion | flops 237633536 | bytes 71680 | tf_op jit(solution)/shard_map/while/body/eval_jaxpr/dot_general | solution.py:43
  593.0 11.5 %fusion.75 = f32[1,3,1792]{2,1,0:T(4,128)S(1)} fusion(f32[3,3584]{1,0:T(4,128)S(1)} %get-tuple-element.283, s32[1792]{0:T(1024)S(1)} %dynamic-slice_reduce_fusion.7), kind=kOutput, calls=%fused_computation.9.clone.1 | convolution fusion | flops 237633536 | bytes 71680 | tf_op jit(solution)/shard_map/while/body/eval_jaxpr/dot_general | solution.py:43
  605.7 11.5 %fusion.75 = f32[1,3,1792]{2,1,0:T(4,128)S(1)} fusion(f32[3,3584]{1,0:T(4,128)S(1)} %get-tuple-element.283, s32[1792]{0:T(1024)S(1)} %dynamic-slice_reduce_fusion.7), kind=kOutput, calls=%fused_computation.9.clone.1 | convolution fusion | flops 237633536 | bytes 71680 | tf_op jit(solution)/shard_map/while/body/eval_jaxpr/dot_general | solution.py:43
  617.6 14.2 %multiply_multiply_fusion = f32[17920,128]{1,0:T(8,128)} fusion(f32[17920,128]{1,0:T(8,128)} %get-tuple-element.152, f32[17920,128]{1,0:T(8,128)} %get-tuple-element.150, f32[17920]{0:T(1024)S(1)} %get-tuple-element.129), kind=kLoop, calls=%fused_computation.28 | loop fusion | flops 4587520 | bytes 27596800 | tf_op jit(solution)/shard_map/mul | solution.py:173
  631.8 11.0 %reshape.347 = f32[896,20,128]{2,1,0:T(8,128)} reshape(f32[17920,128]{1,0:T(8,128)} %multiply_multiply_fusion) | data formatting | bytes 18350080 | tf_op jit(solution)/shard_map/reshape | solution.py:173
  642.8 6.0 reduce_sum.86
  649.2 4.9 broadcast_in_dim.102
  654.0 11.0 %reshape.348 = f32[17920,128]{1,0:T(8,128)} reshape(f32[896,20,128]{2,1,0:T(8,128)} %broadcast_in_dim.102) | data formatting | bytes 18350080 | tf_op jit(solution)/shard_map/reshape | solution.py:85
  665.1 20.2 %fusion.17 = f32[256,128]{1,0:T(8,128)S(1)} fusion(f32[256]{0:T(256)S(1)} %iota_multiply_fusion, f32[17920]{0:T(1024)S(1)} %copy-done.7, f32[17920,128]{1,0:T(8,128)} %get-tuple-element.150, f32[17920,128]{1,0:T(8,128)} %reshape.348, f32[17920]{0:T(1024)S(1)} %fusion.46), kind=kOutput, calls=%fused_computation.33 | convolution fusion | flops 1199636480 | bytes 18625536 | tf_op jit(solution)/shard_map/dot_general | solution.py:179
  685.4 26.0 %fusion.23 = f32[128,128]{1,0:T(8,128)S(1)} fusion(f32[17920,128]{1,0:T(8,128)} %fusion.19, f32[17920,128]{1,0:T(8,128)} %get-tuple-element.152, f32[17920,128]{1,0:T(8,128)} %reshape.345, f32[17920,128]{1,0:T(8,128)S(1)} %copy-done.2, f32[17920]{0:T(1024)S(1)} %get-tuple-element.128, f32[17920]{0:T(1024)S(1)} %fusion.46, ...), kind=kOutput, calls=%fused_computation.38 | convolution fusion | flops 603258880 | bytes 41514496 | tf_op jit(solution)/shard_map/dot_general | solution.py:182
  711.5 19.3 %fusion.26 = f32[256,128]{1,0:T(8,128)S(1)} fusion(f32[256,128]{1,0:T(8,128)S(1)} %fusion.17, f32[17920,128]{1,0:T(8,128)S(1)} %bitcast.95, f32[17920,128]{1,0:T(8,128)S(1)} %bitcast.93, f32[17920]{0:T(1024)S(1)} %get-tuple-element.128, f32[256]{0:T(256)S(1)} %iota_multiply_fusion, f32[17920]{0:T(1024)S(1)} %copy-done.7), kind=kOutput, calls=%fused_computation.43 | convolution fusion | flops 1208844288 | bytes 18756608 | tf_op jit(solution)/shard_map/dot_general | solution.py:179
  732.8 66.0 %all-reduce = (f32[128]{0:T(128)}, f32[]{:T(128)}) all-reduce(f32[128]{0:T(128)S(1)} %get-tuple-element.136, f32[]{:T(128)S(6)} %mul_shard_map.3), channel_id=1, replica_groups=mesh['dp'=8,'graph'=16] {'dp','graph'}, use_global_device_ids=true, to_apply=%region_15.16 | all-reduce | flops 129 | bytes 1032 | tf_op jit(solution)/shard_map/psum | solution.py:184
  798.8 74.9 %all-reduce.3.cloned.1.call-done = f32[384,128]{1,0:T(8,128)} async-done(((f32[384,128]{1,0:T(8,128)}), f32[384,128]{1,0:T(8,128)}) %all-reduce.3.cloned.1.call-update) | async-done | bytes 196624 | tf_op jit(solution)/shard_map/psum | solution.py:184
  873.7 1.6 slice.26
  875.2 1.5 slice.27
  (178 shorter events, 48.4 us)
Async XLA Ops:
  7.2 157.2 %copy-start = (bf16[256,128]{1,0:T(8,128)(2,1)S(1)}, bf16[256,128]{1,0:T(8,128)(2,1)}, u32[]{:S(2)}) copy-start(bf16[256,128]{1,0:T(8,128)(2,1)} %param.23) | copy-start | bytes 196612
  7.2 167.0 %all-gather.3.cloned.1.call-start = ((), (), s32[]{:S(2)}) async-start(), calls=%async_computation.1 | async-start | bytes 3899392 | tf_op jit(solution)/shard_map/all_gather | solution.py:136
  9.9 456.3 %reduce-scatter.4.cloned.1.call-start = ((), (), s32[]{:S(2)}) async-start(), calls=%async_computation.3 | async-start | bytes 7798784
  40.6 122.9 %copy-start.10 = (f32[128]{0:T(128)S(1)}, f32[128]{0:T(128)}, u32[]{:S(2)}) copy-start(f32[128]{0:T(128)} %param.25) | copy-start | bytes 1540
  159.2 0.6 copy-start.3
  161.2 13.0 %copy-start.5 = (f32[17920]{0:T(1024)}, f32[17920]{0:T(1024)S(1)}, u32[]{:S(2)}) copy-start(f32[17920]{0:T(1024)S(1)} %sqrt.20) | copy-start | bytes 215044
  164.4 11.2 %copy-start.4 = (s32[18432]{0:T(1024)S(1)}, s32[18432]{0:T(1024)}, u32[]{:S(2)}) copy-start(s32[18432]{0:T(1024)} %pad_clamp_fusion) | copy-start | bytes 221188
  175.6 36.7 %copy-start.8 = (bf16[128,128]{1,0:T(8,128)(2,1)S(1)}, bf16[128,128]{1,0:T(8,128)(2,1)}, u32[]{:S(2)}) copy-start(bf16[128,128]{1,0:T(8,128)(2,1)} %param.24) | copy-start | bytes 98308
  251.9 11.0 %copy-start.6 = (f32[17920]{0:T(1024)S(1)}, f32[17920]{0:T(1024)}, u32[]{:S(2)}) copy-start(f32[17920]{0:T(1024)} %copy-done.5) | copy-start | bytes 215044
  394.2 73.2 %copy-start.9 = (f32[1,3,896]{2,0,1:T(1,128)S(1)}, f32[1,3,896]{2,0,1:T(1,128)}, u32[]{:S(2)}) copy-start(f32[1,3,896]{2,0,1:T(1,128)} %param.19) | copy-start | bytes 32260
  398.9 474.8 %all-reduce.3.cloned.1.call-start = ((), (), s32[]{:S(2)}) async-start(), calls=%async_computation.2 | async-start | bytes 393216 | tf_op jit(solution)/shard_map/psum | solution.py:184
  654.0 11.0 %copy-start.7 = (f32[17920]{0:T(1024)S(1)}, f32[17920]{0:T(1024)}, u32[]{:S(2)}) copy-start(f32[17920]{0:T(1024)} %copy-done.5) | copy-start | bytes 215044
  654.0 31.3 %slice-start = ((s8[4587520]{0:T(1024)(128)(4,1)}), s8[393216]{0:T(1024)(128)(4,1)S(1)}, s32[]{:S(2)}) async-start(s8[4587520]{0:T(1024)(128)(4,1)} %bitcast.90), calls=%async_computation.4 | async-start | bytes 786432
  665.0 20.3 %slice-start.1 = ((s8[4587520]{0:T(1024)(128)(4,1)}), s8[4194304]{0:T(1024)(128)(4,1)S(1)}, s32[]{:S(2)}) async-start(s8[4587520]{0:T(1024)(128)(4,1)} %bitcast.90), calls=%async_computation.5 | async-start | bytes 8388608
  665.0 20.3 %copy-start.2 = (f32[17920,128]{1,0:T(8,128)S(1)}, f32[17920,128]{1,0:T(8,128)}, u32[]{:S(2)}) copy-start(f32[17920,128]{1,0:T(8,128)} %reshape.348) | copy-start | bytes 27525124
  665.0 46.4 %slice-start.2 = ((s8[9175040]{0:T(1024)(128)(4,1)}), s8[4194304]{0:T(1024)(128)(4,1)S(1)}, s32[]{:S(2)}) async-start(s8[9175040]{0:T(1024)(128)(4,1)} %bitcast.92), calls=%async_computation.6 | async-start | bytes 8388608
  665.0 46.4 %slice-start.3 = ((s8[9175040]{0:T(1024)(128)(4,1)}), s8[4194304]{0:T(1024)(128)(4,1)S(1)}, s32[]{:S(2)}) async-start(s8[9175040]{0:T(1024)(128)(4,1)} %bitcast.92), calls=%async_computation.7 | async-start | bytes 8388608
  665.0 46.4 %slice-start.5 = ((s8[9175040]{0:T(1024)(128)(4,1)}), s8[4194304]{0:T(1024)(128)(4,1)S(1)}, s32[]{:S(2)}) async-start(s8[9175040]{0:T(1024)(128)(4,1)} %bitcast.94), calls=%async_computation.9 | async-start | bytes 8388608
  665.1 46.4 %slice-start.6 = ((s8[9175040]{0:T(1024)(128)(4,1)}), s8[4194304]{0:T(1024)(128)(4,1)S(1)}, s32[]{:S(2)}) async-start(s8[9175040]{0:T(1024)(128)(4,1)} %bitcast.94), calls=%async_computation.10 | async-start | bytes 8388608
  685.4 26.1 %slice-start.4 = ((s8[9175040]{0:T(1024)(128)(4,1)}), s8[786432]{0:T(1024)(128)(4,1)S(1)}, s32[]{:S(2)}) async-start(s8[9175040]{0:T(1024)(128)(4,1)} %bitcast.92), calls=%async_computation.8 | async-start | bytes 1572864
  685.4 26.1 %slice-start.7 = ((s8[9175040]{0:T(1024)(128)(4,1)}), s8[786432]{0:T(1024)(128)(4,1)S(1)}, s32[]{:S(2)}) async-start(s8[9175040]{0:T(1024)(128)(4,1)} %bitcast.94), calls=%async_computation.11 | async-start | bytes 1572864
  711.5 165.2 %copy-start.1 = (bf16[256,128]{1,0:T(8,128)(2,1)S(1)}, bf16[256,128]{1,0:T(8,128)(2,1)}, u32[]{:S(2)}) copy-start(bf16[256,128]{1,0:T(8,128)(2,1)} %param.23) | copy-start | bytes 196612
Sparse Core Ops, SparseCore 0:
  10.0 40.5 all-gather.2
  399.0 67.1 reduce-scatter.3
  731.6 142.0 all-reduce.2
where the time goes:
time: 891 us; the launch traced here: 883 us
  matrix products  434 us (49%)
  local copies, waits for them, and re-layouts  144 us (16%)
  waiting for transfers between devices  140 us (16%)
  blocking collectives  110 us (12%)
  other arithmetic  37.5 us (4%)
  between operations  15.9 us (2%)
    dot_general x20, matrix products, one_block(): lax.dot_general(table, select, (((1,), (1,)), ((), ())), precision=lax.Pr...  230 us
    dot_general x10, matrix products, add_block(): jnp.dot(value_block, select, precision=lax.Precision.HIGHEST, preferred_e...  94.9 us
    psum x1, waiting for transfers between devices, local(): lax.psum((stacked, grad_out_part, loss_part), ('dp', 'graph'))  74.9 us
    psum x1, blocking collectives, local(): lax.psum((stacked, grad_out_part, loss_part), ('dp', 'graph'))  66 us
    unnamed x4, waiting for transfers between devices  65.3 us
    gather x1, local copies, waits for them, and re-layouts, local(): source_rows = jnp.take(every_state, picked, axis=0)  36.7 us
    dot_general x1, matrix products, local(): jnp.dot(source_rows.T, dquery, preferred_element_type=jnp.float32)  26 us
    all_gather x1, blocking collectives, local(): gathered_place = lax.all_gather(places, 'graph', axis=1, tiled=True)  23.1 us
  transfers between devices with their start and end apart: 3, of which 2 were waited for; matrix products, arithmetic and copies ran while one was open for 16% of the time, Pallas kernels for 0%

commit v1 on v0

v1 whole, which is shorter than its diff:
```python
import functools
import math

import jax
import jax.numpy as jnp
from jax import lax
from jax.experimental import pallas as pl
from jax.experimental.pallas import tpu as pltpu
from jax.sharding import PartitionSpec as P

MESH = pl.DeviceIdType.MESH
F32 = jnp.float32
BF16 = jnp.bfloat16
NT = (((1,), (1,)), ((), ()))
DEG = 20
PAD = 24
LANES = 128
VMEM = pltpu.VMEM
LIMIT = 56 * 1024 * 1024


def partners(groups):
    me = lax.axis_index("graph")
    left = lax.rem(me + groups - 1, groups)
    right = lax.rem(me + 1, groups)
    far = lax.rem(me + groups // 2, groups)
    return left, right, far


def greet(devices):
    barrier = pltpu.get_barrier_semaphore()
    for device in devices:
        pl.semaphore_signal(barrier, inc=1, device_id=device, device_id_type=MESH)
    pl.semaphore_wait(barrier, len(devices))


def send(src, dst, send_sem, recv_sem, device):
    copy = pltpu.make_async_remote_copy(
        src_ref=src,
        dst_ref=dst,
        send_sem=send_sem,
        recv_sem=recv_sem,
        device_id=device,
        device_id_type=MESH,
    )
    copy.start()
    return copy


def halo_kernel(
    groups,
    state_ref,
    types_ref,
    place_ref,
    table_ref,
    out_state,
    out_place,
    own_state,
    own_place,
    send_sem,
    recv_sem,
    local_sem,
):
    nodes = state_ref.shape[0]
    kinds = table_ref.shape[0]
    left, right, far = partners(groups)
    targets = ((left, 2), (right, 0), (far, 3))
    own_place[...] = jnp.zeros_like(own_place)
    for c in range(3):
        for n in range(nodes // LANES):
            own_place[8 * c + n : 8 * c + n + 1, :] = place_ref[c : c + 1, n * LANES : (n + 1) * LANES]
    onehot = (
        types_ref[...] == lax.broadcasted_iota(jnp.int32, (kinds, nodes), 0)
    ).astype(BF16)
    embedded = lax.dot_general(
        table_ref[...], onehot, (((0,), (0,)), ((), ())), preferred_element_type=F32
    )
    own_state[...] = (state_ref[...].astype(F32).T + embedded).astype(BF16)
    greet([{"graph": left}, {"graph": right}, {"graph": far}])
    copies = []
    for i, (device, slot) in enumerate(targets):
        copies.append(
            send(own_state, out_state.at[slot], send_sem.at[i], recv_sem.at[i], {"graph": device})
        )
        copies.append(
            send(own_place, out_place.at[slot], send_sem.at[3 + i], recv_sem.at[3 + i], {"graph": device})
        )
    first = pltpu.make_async_copy(own_state, out_state.at[1], local_sem.at[0])
    second = pltpu.make_async_copy(own_place, out_place.at[1], local_sem.at[1])
    first.start()
    second.start()
    for copy in copies:
        copy.wait()
    first.wait()
    second.wait()


def lane_pick(row, index):
    return jnp.take_along_axis(
        jnp.broadcast_to(row, index.shape), index, axis=1, mode="promise_in_bounds"
    )


def pick_three(tab_ref, rows, lane, row_of):
    result = [jnp.zeros(lane.shape, F32)] * 3
    for r in range(rows):
        here = row_of == r
        for c in range(3):
            at = (r // 7) * PAD + c * 8 + r % 7
            result[c] = jnp.where(here, lane_pick(tab_ref[at : at + 1, :], lane), result[c])
    return result


def basis(dist_row, scaled_centers, gamma):
    diff = (-2.0 * gamma) * dist_row - scaled_centers
    bump = jnp.exp2(diff * diff * (-math.log2(math.e) / (4.0 * gamma)))
    return bump.astype(BF16), (diff * bump).astype(BF16)


def centers(count):
    gamma = count * count / 1152.0
    number = lax.broadcasted_iota(jnp.int32, (count, LANES), 0).astype(F32)
    return number * (12.0 / count) * (-2.0 * gamma), gamma


def node_terms(agg):
    sig = jax.nn.sigmoid(agg)
    first = sig * (1.0 + agg * (1.0 - sig))
    second = sig * (1.0 - sig) * (2.0 + agg * (1.0 - 2.0 * sig))
    return first, second


STEP = 4


def forward_kernel(
    groups,
    state_ref,
    place_ref,
    source_ref,
    count_ref,
    w_rad_ref,
    w_src_ref,
    w_out_ref,
    rows_ref,
    query_ref,
    slope_ref,
    radial_ref,
    scalar_ref,
    index_ref,
    agg_ref,
    incoming_ref,
    outgoing_ref,
    stack,
    w_rad_t,
    w_src_t,
    w_out_t,
    centre,
    pick,
    onehots,
    product,
    agg_acc,
    spread,
):
    n = pl.program_id(0)
    channels = w_src_ref.shape[0]
    count = w_rad_ref.shape[0]
    gamma = count * count / 1152.0
    me = lax.axis_index("graph")

    @pl.when(n == 0)
    def _():
        w_rad_t[...] = w_rad_ref[...].astype(F32).T.astype(BF16)
        w_src_t[...] = w_src_ref[...].astype(F32).T.astype(BF16)
        w_out_t[...] = jnp.broadcast_to(w_out_ref[...], (channels, LANES)).T
        centre[...] = centers(count)[0]
        spread[...] = jnp.zeros_like(spread)
        incoming_ref[...] = jnp.zeros_like(incoming_ref)
        for half in range(28):
            rows = slice((half // 2) * channels, (half // 2 + 1) * channels)
            at = (half % 7) * LANES
            stack[rows, (half % 2) * LANES : (half % 2 + 1) * LANES] = state_ref[
                half // 7, :, at : at + LANES
            ]

    slot = lax.broadcasted_iota(jnp.int32, (PAD, LANES), 1) * DEG + lax.broadcasted_iota(
        jnp.int32, (PAD, LANES), 0
    )
    lane = slot & (LANES - 1)
    row_of = slot >> 7
    source = jnp.zeros((PAD, LANES), jnp.int32)
    for r in range(DEG):
        source = jnp.where(row_of == r, lane_pick(source_ref[pl.ds(n * DEG + r, 1), :], lane), source)
    nodes = 7 * LANES
    block = (source * 74899) >> 26
    offset = (block - me + groups) & (groups - 1)
    position = jnp.where(
        offset == groups - 1, 0, jnp.where(offset == 0, 1, jnp.where(offset == 1, 2, 3))
    )
    picked = position * nodes + source - block * nodes
    live = slot + n * (DEG * LANES) < count_ref[0, 0]
    lane = picked & (LANES - 1)
    row_of = picked >> 7
    index_ref[0, :PAD] = lane
    index_ref[0, PAD:] = row_of
    source_place = pick_three(place_ref, 28, lane, row_of)
    delta = [
        source_place[c] - place_ref[pl.ds(PAD + 8 * c + n, 1), :] for c in range(3)
    ]
    dist = jnp.sqrt(delta[0] * delta[0] + delta[1] * delta[1] + delta[2] * delta[2] + 0.25)
    unit = [delta[c] / dist for c in range(3)]
    for c in range(3):
        scalar_ref[0, c * PAD : (c + 1) * PAD] = unit[c]
    scalar_ref[0, 3 * PAD :] = dist
    pick[:PAD] = jnp.where(live, (picked & 255).astype(F32), -1.0)
    pick[PAD : 2 * PAD] = (picked >> 8).astype(F32)
    pick[2 * PAD :] = dist
    agg_acc[...] = jnp.zeros_like(agg_acc)
    wide = STEP * LANES

    def piece(i, chunks):
        place = pl.ds(pl.multiple_of(i * wide, wide), wide)
        numbers = lax.broadcasted_iota(jnp.int32, (256, LANES), 0).astype(F32)
        ones, bumps, slants, hi = [], [], [], []
        for j in range(STEP):
            column = pick[pl.ds(i * STEP + j, 1), :]
            ones.append((numbers == column).astype(BF16))
            bump, slant = basis(pick[pl.ds(2 * PAD + i * STEP + j, 1), :], centre[...], gamma)
            bumps.append(bump)
            slants.append(slant)
            hi.append(pick[pl.ds(PAD + i * STEP + j, 1), :])
        ones = jnp.concatenate(ones, axis=1)
        bumps = jnp.concatenate(bumps, axis=1)
        slants = jnp.concatenate(slants, axis=1)
        hi = jnp.broadcast_to(jnp.concatenate(hi, axis=1), (channels, wide))
        onehots[:, place] = ones
        found = jnp.dot(stack[: chunks * channels], ones, preferred_element_type=F32)
        rows = found[:channels]
        for c in range(1, chunks):
            rows = jnp.where(hi == float(c), found[c * channels : (c + 1) * channels], rows)
        rows = rows.astype(BF16)
        rows_ref[0, :, place] = rows
        query = jnp.dot(w_src_t[...], rows, preferred_element_type=F32)
        radial = jnp.dot(w_rad_t[...], bumps, preferred_element_type=F32)
        slope = jnp.dot(w_rad_t[...], slants, preferred_element_type=F32)
        query_ref[0, :, place] = query.astype(BF16)
        slope_ref[0, :, place] = slope.astype(BF16)
        radial_ref[0, :, place] = radial.astype(BF16)
        product[:, place] = query * slope
        term = radial * query
        total = term[:, :LANES]
        for j in range(1, STEP):
            total = total + term[:, j * LANES : (j + 1) * LANES]
        agg_acc[...] += total

    @pl.when(n == 0)
    def _():
        lax.fori_loop(0, DEG // STEP, lambda i, u: (piece(i, 14), u)[1], 0)

    @pl.when(n > 0)
    def _():
        lax.fori_loop(0, DEG // STEP, lambda i, u: (piece(i, 11), u)[1], 0)

    agg = 0.2 * agg_acc[...]
    agg_ref[0] = agg
    first, _ = node_terms(agg)
    readout = 0.2 * first * w_out_t[...]
    incoming = [jnp.zeros((1, LANES), F32)] * 3
    lhs = []
    chunk = lax.broadcasted_iota(jnp.int32, (16, LANES), 0).astype(F32)
    for j in range(DEG):
        pull = jnp.sum(readout * product[:, j * LANES : (j + 1) * LANES], axis=0, keepdims=True)
        here = chunk == pick[PAD + j : PAD + j + 1, :]
        high, low = [], []
        for c in range(3):
            moved = pull * scalar_ref[0, c * PAD + j : c * PAD + j + 1, :]
            incoming[c] = incoming[c] + moved
            term = jnp.where(here, moved, 0.0)
            top = term.astype(BF16)
            high.append(top)
            low.append((term - top.astype(F32)).astype(BF16))
        lhs.append(jnp.concatenate(high + low, axis=0))
    lhs = jnp.concatenate(lhs, axis=1)
    spread[...] += lax.dot_general(lhs, onehots[...], NT, preferred_element_type=F32)
    for c in range(3):
        incoming_ref[pl.ds(8 * c + n, 1), :] = incoming[c]

    @pl.when(n == 6)
    def _():
        outgoing_ref[...] = jnp.zeros_like(outgoing_ref)
        total = spread[:48] + spread[48:]
        for c in range(3):
            for r in range(28):
                at = (r // 7) * PAD + c * 8 + r % 7
                outgoing_ref[at : at + 1, :] = total[
                    c * 16 + r // 2 : c * 16 + r // 2 + 1, (r % 2) * LANES : (r % 2 + 1) * LANES
                ]


def force_kernel(
    groups,
    weight_loss,
    outgoing_ref,
    incoming_ref,
    wanted_ref,
    forces_ref,
    back_ref,
    loss_ref,
    terms,
    mine,
    wanted,
    tables,
    send_sem,
    recv_sem,
):
    left, right, far = partners(groups)
    greet([{"graph": left}, {"graph": right}, {"graph": far}])
    copies = []
    for i, (device, slot) in enumerate(((left, 0), (right, 2), (far, 3))):
        copies.append(
            send(
                outgoing_ref.at[slot * PAD : (slot + 1) * PAD],
                terms.at[i],
                send_sem.at[i],
                recv_sem.at[i],
                {"graph": device},
            )
        )
    wanted[...] = jnp.zeros_like(wanted)
    for c in range(3):
        for n in range(7):
            wanted[8 * c + n : 8 * c + n + 1, :] = wanted_ref[c : c + 1, n * LANES : (n + 1) * LANES]
    for copy in copies:
        copy.wait()
    forces = incoming_ref[...] - (outgoing_ref[PAD : 2 * PAD] + terms[0] + terms[1] + terms[2])
    miss = forces - wanted[...]
    mine[...] = 2.0 * weight_loss * miss
    copies = []
    for i, device in enumerate((left, right, far)):
        copies.append(
            send(mine, tables.at[i], send_sem.at[3 + i], recv_sem.at[3 + i], {"graph": device})
        )
    for c in range(3):
        for n in range(7):
            forces_ref[c : c + 1, n * LANES : (n + 1) * LANES] = forces[8 * c + n : 8 * c + n + 1, :]
    square = miss * miss
    total = weight_loss * jnp.sum(square, axis=(0, 1), keepdims=True)
    loss_ref[...] = jnp.broadcast_to(total, loss_ref.shape)
    back_ref[PAD : 2 * PAD] = mine[...]
    for copy in copies:
        copy.wait()
    back_ref[2 * PAD : 3 * PAD] = tables[0]
    back_ref[:PAD] = tables[1]
    back_ref[3 * PAD :] = tables[2]


def backward_kernel(
    back_ref,
    scalar_ref,
    index_ref,
    agg_ref,
    rows_ref,
    query_ref,
    slope_ref,
    radial_ref,
    w_out_ref,
    grads_ref,
    w_out_t,
    centre,
    lam_ref,
    coefs,
    bases,
    wants,
    grad_radial,
    grad_source,
    grad_out,
):
    n = pl.program_id(0)
    channels = rows_ref.shape[1]
    count = centre.shape[0]
    gamma = count * count / 1152.0

    @pl.when(n == 0)
    def _():
        w_out_t[...] = jnp.broadcast_to(w_out_ref[...], (channels, LANES)).T
        centre[...] = centers(count)[0]
        grad_radial[...] = jnp.zeros_like(grad_radial)
        grad_source[...] = jnp.zeros_like(grad_source)
        grad_out[...] = jnp.zeros_like(grad_out)

    lane = index_ref[0, :PAD]
    row_of = index_ref[0, PAD:]
    source_back = pick_three(back_ref, 28, lane, row_of)
    lam = jnp.zeros((PAD, LANES), F32)
    for c in range(3):
        lam = lam + (back_ref[pl.ds(PAD + 8 * c + n, 1), :] - source_back[c]) * scalar_ref[
            0, c * PAD : (c + 1) * PAD
        ]
    lam_ref[...] = 0.2 * lam
    first, second = node_terms(agg_ref[0])
    w_out = w_out_t[...]
    readout = first * w_out

    def gather(j, total):
        place = pl.ds(pl.multiple_of(j * LANES, LANES), LANES)
        return total + lam_ref[pl.ds(j, 1), :] * (
            query_ref[0, :, place].astype(F32) * slope_ref[0, :, place].astype(F32)
        )

    dread = lax.fori_loop(0, DEG, gather, jnp.zeros((channels, LANES), F32))
    grad_out[...] += dread * first
    plain = 0.2 * dread * w_out * second

    def piece(j, unused):
        place = pl.ds(pl.multiple_of(j * LANES, LANES), LANES)
        later = pl.ds(pl.multiple_of((DEG + j) * LANES, LANES), LANES)
        bump, slant = basis(scalar_ref[0, pl.ds(3 * PAD + j, 1), :], centre[...], gamma)
        bases[:, place] = bump
        bases[:, later] = slant
        over_slope = lam_ref[pl.ds(j, 1), :] * readout
        query = query_ref[0, :, place].astype(F32)
        coefs[:, place] = (plain * query).astype(BF16)
        coefs[:, later] = (over_slope * query).astype(BF16)
        wants[:, place] = (
            over_slope * slope_ref[0, :, place].astype(F32)
            + plain * radial_ref[0, :, place].astype(F32)
        ).astype(BF16)
        return unused

    lax.fori_loop(0, DEG, piece, 0)
    grad_radial[...] += lax.dot_general(coefs[...], bases[...], NT, preferred_element_type=F32)
    grad_source[...] += lax.dot_general(rows_ref[0], wants[...], NT, preferred_element_type=F32)

    @pl.when(n == 6)
    def _():
        radial = grad_radial[...].T
        source = grad_source[...]
        out = jnp.sum(grad_out[...].T, axis=0, keepdims=True)
        for i in range(16):
            for k in range(3):
                at = (3 * i + k) * 8
                grads_ref[i, 8 * k : 8 * k + 8] = (
                    radial[at : at + 8] if at < count else source[at - count : at - count + 8]
                )
            grads_ref[i, 24:] = jnp.zeros((8, LANES), F32)
        grads_ref[0, 24:25] = out


def sum_kernel(
    groups,
    batches,
    grads_ref,
    loss_ref,
    radial_ref,
    source_ref,
    out_ref,
    total_loss_ref,
    first,
    part,
    whole,
    own,
    send_sem,
    recv_sem,
    dp_send,
    dp_recv,
    back_send,
    back_recv,
):
    me = lax.axis_index("graph")
    batch = lax.axis_index("dp")
    peers = [lax.rem(me + d, groups) for d in range(1, groups)]
    others = [lax.rem(batch + d, batches) for d in range(1, batches)]
    own[...] = grads_ref[...]
    own[0, 25:26] = loss_ref[0:1, :]
    greet([{"graph": p} for p in peers] + [{"dp": b} for b in others])
    copies = []
    for i, p in enumerate(peers):
        copies.append(send(own.at[p], first.at[i], send_sem.at[i], recv_sem.at[i], {"graph": p}))
    for copy in copies:
        copy.wait()
    total = own[me]
    for i in range(groups - 1):
        total = total + first[i]
    part[batch] = total
    copies = []
    for i, b in enumerate(others):
        copies.append(send(part.at[batch], part.at[batch], dp_send.at[i], dp_recv.at[i], {"dp": b}))
    for copy in copies:
        copy.wait()
    total = part[0]
    for i in range(1, batches):
        total = total + part[i]
    whole[me] = total
    copies = []
    for i, p in enumerate(peers):
        copies.append(send(whole.at[me], whole.at[me], back_send.at[i], back_recv.at[i], {"graph": p}))
    for copy in copies:
        copy.wait()
    count = radial_ref.shape[0]
    for i in range(groups):
        for k in range(3):
            at = (3 * i + k) * 8
            if at < count:
                radial_ref[at : at + 8] = whole[i, 8 * k : 8 * k + 8]
            else:
                source_ref[at - count : at - count + 8] = whole[i, 8 * k : 8 * k + 8]
    out_ref[...] = whole[0, 24:25]
    total_loss_ref[...] = whole[0, 25:26]


def whole_vmem():
    return pl.BlockSpec(memory_space=VMEM)


def local(
    node_state,
    atom_types,
    positions,
    force_ref,
    edge_source,
    edge_count,
    type_table,
    w_rad,
    w_src,
    w_out,
):
    nodes, channels = node_state.shape[1:]
    groups = lax.axis_size("graph")
    batches = lax.axis_size("dp")
    weight_loss = 1.0 / math.sqrt(3.0 * nodes * groups * node_state.shape[0] * batches)
    count = w_rad.shape[0]
    tiles = nodes // LANES
    wide = DEG * LANES
    dma = pltpu.SemaphoreType.DMA
    any_space = pl.BlockSpec(memory_space=pl.ANY)

    def shape(*dims, dtype=F32):
        return jax.ShapeDtypeStruct(dims, dtype)

    state, place = pl.pallas_call(
        functools.partial(halo_kernel, groups),
        out_shape=(shape(4, channels, nodes, dtype=BF16), shape(4, PAD, LANES)),
        in_specs=[whole_vmem()] * 4,
        out_specs=(any_space, any_space),
        scratch_shapes=[
            VMEM((channels, nodes), BF16),
            VMEM((PAD, LANES), F32),
            dma((6,)),
            dma((6,)),
            dma((2,)),
        ],
        compiler_params=pltpu.CompilerParams(collective_id=0, has_side_effects=True),
        name="halo",
    )(node_state[0], atom_types, positions[0], type_table)

    tile = lambda *dims: pl.BlockSpec((1,) + dims, lambda n: (n,) + (0,) * len(dims))
    fixed = lambda *dims: pl.BlockSpec(dims, lambda n: (0,) * len(dims))
    rows, query, slope, radial, scalar, index, agg, incoming, outgoing = pl.pallas_call(
        functools.partial(forward_kernel, groups),
        grid=(tiles,),
        out_shape=(
            *[shape(tiles, channels, wide, dtype=BF16)] * 4,
            shape(tiles, 4 * PAD, LANES),
            shape(tiles, 2 * PAD, LANES, dtype=jnp.int32),
            shape(tiles, channels, LANES),
            shape(PAD, LANES),
            shape(4 * PAD, LANES),
        ),
        in_specs=[
            fixed(4, channels, nodes),
            fixed(4 * PAD, LANES),
            fixed(DEG * tiles, LANES),
            pl.BlockSpec(memory_space=pltpu.SMEM),
            fixed(count, channels),
            fixed(channels, channels),
            fixed(1, channels),
        ],
        out_specs=(
            *[tile(channels, wide)] * 4,
            tile(4 * PAD, LANES),
            tile(2 * PAD, LANES),
            tile(channels, LANES),
            fixed(PAD, LANES),
            fixed(4 * PAD, LANES),
        ),
        scratch_shapes=[
            VMEM((14 * channels, 256), BF16),
            VMEM((channels, count), BF16),
            VMEM((channels, channels), BF16),
            VMEM((channels, LANES), F32),
            VMEM((count, LANES), F32),
            VMEM((3 * PAD, LANES), F32),
            VMEM((256, wide), BF16),
            VMEM((channels, wide), F32),
            VMEM((channels, LANES), F32),
            VMEM((96, 256), F32),
        ],
        compiler_params=pltpu.CompilerParams(vmem_limit_bytes=LIMIT),
        name="forward",
    )(
        state,
        place.reshape(4 * PAD, LANES),
        edge_source.reshape(DEG * tiles, LANES),
        edge_count,
        w_rad,
        w_src,
        w_out.reshape(1, channels),
    )

    forces, back, loss = pl.pallas_call(
        functools.partial(force_kernel, groups, weight_loss),
        out_shape=(shape(3, nodes), shape(4 * PAD, LANES), shape(8, LANES)),
        in_specs=[whole_vmem()] * 3,
        out_specs=(whole_vmem(),) * 3,
        scratch_shapes=[
            VMEM((3, PAD, LANES), F32),
            VMEM((PAD, LANES), F32),
            VMEM((PAD, LANES), F32),
            VMEM((3, PAD, LANES), F32),
            dma((6,)),
            dma((6,)),
        ],
        compiler_params=pltpu.CompilerParams(collective_id=1, has_side_effects=True),
        name="force",
    )(outgoing, incoming, force_ref[0])

    grads = pl.pallas_call(
        backward_kernel,
        grid=(tiles,),
        out_shape=shape(16, 32, LANES),
        in_specs=[
            fixed(4 * PAD, LANES),
            tile(4 * PAD, LANES),
            tile(2 * PAD, LANES),
            tile(channels, LANES),
            *[tile(channels, wide)] * 4,
            fixed(1, channels),
        ],
        out_specs=fixed(16, 32, LANES),
        scratch_shapes=[
            VMEM((channels, LANES), F32),
            VMEM((count, LANES), F32),
            VMEM((PAD, LANES), F32),
            VMEM((channels, 2 * wide), BF16),
            VMEM((count, 2 * wide), BF16),
            VMEM((channels, wide), BF16),
            VMEM((channels, count), F32),
            VMEM((channels, channels), F32),
            VMEM((channels, LANES), F32),
        ],
        compiler_params=pltpu.CompilerParams(vmem_limit_bytes=LIMIT),
        name="backward",
    )(back, scalar, index, agg, rows, query, slope, radial, w_out.reshape(1, channels))

    grad_radial, grad_source, grad_out, total_loss = pl.pallas_call(
        functools.partial(sum_kernel, groups, batches),
        out_shape=(
            shape(count, channels),
            shape(channels, channels),
            shape(1, channels),
            shape(1, LANES),
        ),
        in_specs=[whole_vmem()] * 2,
        out_specs=(whole_vmem(),) * 4,
        scratch_shapes=[
            VMEM((groups - 1, 32, LANES), F32),
            VMEM((batches, 32, LANES), F32),
            VMEM((groups, 32, LANES), F32),
            VMEM((groups, 32, LANES), F32),
            dma((groups - 1,)),
            dma((groups - 1,)),
            dma((max(batches - 1, 1),)),
            dma((max(batches - 1, 1),)),
            dma((groups - 1,)),
            dma((groups - 1,)),
        ],
        compiler_params=pltpu.CompilerParams(collective_id=2, has_side_effects=True),
        name="total",
    )(grads, loss)
    return forces[None], grad_radial, grad_source, grad_out[0], total_loss[0, 0]


def solution(mesh):
    in_specs = (
        P("dp", "graph", None),
        P("dp", "graph"),
        P("dp", None, "graph"),
        P("dp", None, "graph"),
        P("dp", "graph"),
        P("dp", "graph"),
        P(),
        P(),
        P(),
        P(),
    )
    out_specs = (P("dp", None, "graph"), P(), P(), P(), P())
    return jax.shard_map(local, mesh=mesh, in_specs=in_specs, out_specs=out_specs, check_vma=False)
```

time: 891 us -> 133 us (0.15)
  matrix products: 434 us -> 0 us
  waiting for transfers between devices: 140 us -> 0 us
  local copies, waits for them, and re-layouts: 144 us -> 7.45 us
  Pallas kernels: 0 us -> 121 us
  blocking collectives: 110 us -> 0 us
  other arithmetic: 37.5 us -> 1.69 us
  between operations: 15.9 us -> 3.01 us
    dot_general x37 -> x0, matrix products: 434 us -> none  [the longest x20 230 us: one_block(): lax.dot_general(table, select, (((1,), (1,)), ((), ())), precision=lax.Pr...]
    pallas_call x0 -> x5, Pallas kernels: none -> 121 us  [the longest x1 43.8 us: local(): pl.pallas_call(functools.partial(forward_kernel, groups), grid=(tiles,),...]
    psum x1 -> x0, waiting for transfers between devices: 74.9 us -> none  [local(): lax.psum((stacked, grad_out_part, loss_part), ('dp', 'graph'))]
    psum x1 -> x0, blocking collectives: 66 us -> none  [local(): lax.psum((stacked, grad_out_part, loss_part), ('dp', 'graph'))]
    unnamed x4 -> x0, waiting for transfers between devices: 65.3 us -> none
    reshape x6 -> x0, local copies, waits for them, and re-layouts: 46.5 us -> none  [the longest x2 21.9 us: widen_rows(): jnp.broadcast_to(values[:, None, :], (nodes, degree, values.shape[1]))]
    all_gather x2 -> x0, blocking collectives: 44.2 us -> none  [the longest x1 23.1 us: local(): gathered_place = lax.all_gather(places, 'graph', axis=1, tiled=True)]
    gather x1 -> x0, local copies, waits for them, and re-layouts: 36.7 us -> none  [local(): source_rows = jnp.take(every_state, picked, axis=0)]
  transfers between devices with their start and end apart: 3 -> 0, of which waited for: 2 -> 0; matrix products, arithmetic and copies ran while one was open for 16% -> 0% of each run, Pallas kernels for 0% -> 0%
where the time goes in v1:
time: 133 us
  Pallas kernels  121 us (91%)
  local copies, waits for them, and re-layouts  7.45 us (6%)
  between operations  3.01 us (2%)
  other arithmetic  1.69 us (1%)
    pallas_call x1, Pallas kernels, local(): pl.pallas_call(functools.partial(forward_kernel, groups), grid=(tiles,),...  43.8 us
    pallas_call x1, Pallas kernels, local(): pl.pallas_call(backward_kernel, grid=(tiles,), out_shape=shape(16, 32, LA...  30.1 us
    pallas_call x1, Pallas kernels, local(): pl.pallas_call(functools.partial(sum_kernel, groups, batches), out_shape=...  24.1 us
    pallas_call x1, Pallas kernels, local(): pl.pallas_call(functools.partial(force_kernel, groups, weight_loss), out_...  12.4 us
    pallas_call x1, Pallas kernels, local(): pl.pallas_call(functools.partial(halo_kernel, groups), out_shape=(shape(4...  10.1 us
    unnamed x8, local copies, waits for them, and re-layouts  7.45 us

profile of v1, /device:TPU:1, one launch (start us, length us, event | category | flops | bytes accessed | tf_op | source)
XLA Modules:
  0.0 132.7 jit_solution(7525895396739024186)
XLA Ops:
  0.6 1.3 copy.21
  1.9 10.1 %halo.1 = (bf16[4,128,896]{2,1,0:T(8,128)(2,1)}, f32[4,24,128]{2,1,0:T(8,128)}) custom-call(bf16[896,128]{1,0:T(8,128)(2,1)} %bitcast.15, s32[1,896]{1,0:T(1,128)} %types_ref.1, f32[3,896]{1,0:T(4,128)} %bitcast.17, bf16[90,128]{1,0:T(8,128)(2,1)} %table_ref.1), custom_call_target="tpu_custom_call" | custom-call | tf_op jit(solution)/shard_map/halo/pallas_call | solution.py:540
  12.1 1.7 %reduce = s32[17920]{0:T(1024)} reduce(s32[1,17920]{1,0:T(1,128)} %param.14, s32[]{:T(128)} %constant.6), dimensions={0}, to_apply=%param.14.reduce_sub_computation | reduce | bytes 143364 | tf_op args[4]
  14.4 43.8 %forward.1 = (bf16[7,128,2560]{2,1,0:T(8,128)(2,1)}, bf16[7,128,2560]{2,1,0:T(8,128)(2,1)}, bf16[7,128,2560]{2,1,0:T(8,128)(2,1)}, bf16[7,128,2560]{2,1,0:T(8,12...) custom-call(bf16[4,128,896]{2,1,0:T(8,128)(2,1)} %get-tuple-element., ...), custom_call_target="tpu_custom_call" | custom-call | tf_op jit(solution)/shard_map/forward/pallas_call | solution.py:558
  58.2 1.3 copy.20
  59.5 12.4 %force.1 = (f32[3,896]{1,0:T(4,128)}, f32[96,128]{1,0:T(8,128)}, f32[8,128]{1,0:T(8,128)}) custom-call(f32[96,128]{1,0:T(8,128)} %get-tuple-element.25.outgoing_ref, f32[24,128]{1,0:T(8,128)} %get-tuple-element.26.incoming_ref, f32[3,896]{1,0:T(4,128)} %bitcast.16), custom_call_target="tpu_custom_call" | custom-call | tf_op jit(solution)/shard_map/force/pallas_call | solution.py:610
  72.0 0.0 copy-start
  72.0 30.1 %backward.1.grads_ref = f32[16,32,128]{2,1,0:T(8,128)} custom-call(f32[96,128]{1,0:T(8,128)} %get-tuple-element.28.back_ref, f32[7,96,128]{2,1,0:T(8,128)} %get-tuple-element.29.scalar_ref, s32[7,48,128]{2,1,0:T(8,128)} %get-tuple-element.30.index_ref, f32[7,128,128]{2,1,0:T(8,128)} %get-tuple-element.31.agg_ref, ...), custom_call_target="tpu_custom_call" | custom-call | tf_op jit(solution)/shard_map/backward/pallas_call | solution.py:627
  102.1 24.1 %total.1 = (f32[256,128]{1,0:T(8,128)}, f32[128,128]{1,0:T(8,128)}, f32[1,128]{1,0:T(1,128)}, f32[1,128]{1,0:T(1,128)}) custom-call(f32[16,32,128]{2,1,0:T(8,128)} %backward.1.grads_ref, f32[8,128]{1,0:T(8,128)} %get-tuple-element.36.loss_ref), custom_call_target="tpu_custom_call" | custom-call | tf_op jit(solution)/shard_map/total/pallas_call | solution.py:655
  126.2 0.0 copy-done
  126.2 0.6 copy.15
  126.8 1.6 %copy.27 = f32[256,128]{1,0:T(8,128)} copy(f32[256,128]{1,0:T(8,128)} %get-tuple-element.52) | data formatting | bytes 262144
  128.4 1.5 %copy.28 = f32[128,128]{1,0:T(8,128)} copy(f32[128,128]{1,0:T(8,128)} %get-tuple-element.53) | data formatting | bytes 131072
  129.8 1.2 copy.29
Async XLA Ops:
  72.0 54.2 %copy-start = (f32[3,896]{1,0:T(4,128)S(1)}, f32[3,896]{1,0:T(4,128)}, u32[]{:S(2)}) copy-start(f32[3,896]{1,0:T(4,128)} %get-tuple-element.27) | copy-start | bytes 32260

commit v2 on v0

v2 whole, which is shorter than its diff:
```python
import functools
import math

import jax
import jax.numpy as jnp
from jax import lax
from jax.experimental import pallas as pl
from jax.experimental.pallas import tpu as pltpu
from jax.sharding import PartitionSpec as P

MESH = pl.DeviceIdType.MESH
F32 = jnp.float32
BF16 = jnp.bfloat16
NT = (((1,), (1,)), ((), ()))
DEG = 20
PAD = 24
LANES = 128
VMEM = pltpu.VMEM
LIMIT = 60 * 1024 * 1024
STEP = 10
WIDE = STEP * LANES


def partners(groups):
    me = lax.axis_index("graph")
    left = lax.rem(me + groups - 1, groups)
    right = lax.rem(me + 1, groups)
    far = lax.rem(me + groups // 2, groups)
    return left, right, far


def greet(devices):
    barrier = pltpu.get_barrier_semaphore()
    for device in devices:
        pl.semaphore_signal(barrier, inc=1, device_id=device, device_id_type=MESH)
    pl.semaphore_wait(barrier, len(devices))


def send(src, dst, send_sem, recv_sem, device):
    copy = pltpu.make_async_remote_copy(
        src_ref=src,
        dst_ref=dst,
        send_sem=send_sem,
        recv_sem=recv_sem,
        device_id=device,
        device_id_type=MESH,
    )
    copy.start()
    return copy


def lane_pick(row, index):
    return jnp.take_along_axis(
        jnp.broadcast_to(row, index.shape), index, axis=1, mode="promise_in_bounds"
    )


def pick_three(tab_ref, rows, lane, row_of):
    result = [jnp.zeros(lane.shape, F32)] * 3
    for r in range(rows):
        here = row_of == r
        for c in range(3):
            at = c * 8 + r % 7
            result[c] = jnp.where(
                here, lane_pick(tab_ref[r // 7, at : at + 1, :], lane), result[c]
            )
    return result


def basis(dist_row, scaled_centers, gamma):
    diff = (-2.0 * gamma) * dist_row - scaled_centers
    bump = jnp.exp2(diff * diff * (-math.log2(math.e) / (4.0 * gamma)))
    return bump.astype(BF16), (diff * bump).astype(BF16)


def centers(count):
    gamma = count * count / 1152.0
    number = lax.broadcasted_iota(jnp.int32, (count, LANES), 0).astype(F32)
    return number * (12.0 / count) * (-2.0 * gamma), gamma


def node_terms(agg):
    sig = jax.nn.sigmoid(agg)
    first = sig * (1.0 + agg * (1.0 - sig))
    second = sig * (1.0 - sig) * (2.0 + agg * (1.0 - 2.0 * sig))
    return first, second


def prepare_indices(groups, source_ref, count_ref, lanes_ref, rows_ref, pick_ref, tiles):
    me = lax.axis_index("graph")
    slot = lax.broadcasted_iota(jnp.int32, (PAD, LANES), 1) * DEG + lax.broadcasted_iota(
        jnp.int32, (PAD, LANES), 0
    )
    lane = slot & (LANES - 1)
    row_of = slot >> 7
    nodes = tiles * LANES
    for n in range(tiles):
        source = jnp.zeros((PAD, LANES), jnp.int32)
        for r in range(DEG):
            at = (n * DEG + r) * LANES
            source = jnp.where(row_of == r, lane_pick(source_ref[:, at : at + LANES], lane), source)
        block = (source * 74899) >> 26
        offset = (block - me + groups) & (groups - 1)
        position = jnp.where(
            offset == groups - 1, 0, jnp.where(offset == 0, 1, jnp.where(offset == 1, 2, 3))
        )
        picked = position * nodes + source - block * nodes
        live = slot + n * (DEG * LANES) < count_ref[...]
        lanes_ref[n] = picked & (LANES - 1)
        rows_ref[n] = picked >> 7
        pick_ref[n, :PAD] = jnp.where(live, (picked & 255).astype(F32), -1.0)
        pick_ref[n, PAD:] = (picked >> 8).astype(F32)


def fused_kernel(
    groups,
    batches,
    weight_loss,
    state_ref,
    types_ref,
    place_ref,
    wanted_ref,
    source_ref,
    count_ref,
    table_ref,
    w_rad_ref,
    w_src_ref,
    w_out_ref,
    forces_ref,
    whole_ref,
    states,
    places,
    stack,
    w_rad_t,
    w_src_t,
    w_out_t,
    centre,
    lanes,
    rows_of,
    pick,
    scalar,
    bumps,
    slants,
    rows_keep,
    query_keep,
    slope_keep,
    radial_keep,
    agg_keep,
    onehots,
    product,
    agg_acc,
    spread,
    incoming,
    outgoing,
    terms,
    wanted,
    backs,
    lam_ref,
    plain_coef,
    slope_coef,
    wants,
    grad_radial,
    grad_source,
    grad_out,
    own,
    pieces,
    part,
    whole,
    halo_send,
    halo_recv,
    term_send,
    term_recv,
    piece_send,
    piece_recv,
    part_send,
    part_recv,
    whole_send,
    whole_recv,
):
    nodes, channels = state_ref.shape
    tiles = nodes // LANES
    kinds = table_ref.shape[0]
    count = w_rad_ref.shape[0]
    gamma = count * count / 1152.0
    me = lax.axis_index("graph")
    batch = lax.axis_index("dp")
    left, right, far = partners(groups)
    near_by = (left, right, far)
    peers = [lax.rem(me + d, groups) for d in range(1, groups)]
    others = [lax.rem(batch + d, batches) for d in range(1, batches)]

    barrier = pltpu.get_barrier_semaphore()
    for device in [{"graph": p} for p in peers] + [{"dp": b} for b in others]:
        pl.semaphore_signal(barrier, inc=1, device_id=device, device_id_type=MESH)

    places[1] = jnp.zeros((PAD, LANES), F32)
    wanted[...] = jnp.zeros_like(wanted)
    for c in range(3):
        for n in range(tiles):
            at = slice(n * LANES, (n + 1) * LANES)
            places[1, 8 * c + n : 8 * c + n + 1, :] = place_ref[c, :, at]
            wanted[8 * c + n : 8 * c + n + 1, :] = wanted_ref[c, :, at]
    kind = (types_ref[...] == lax.broadcasted_iota(jnp.int32, (kinds, nodes), 0)).astype(BF16)
    embedded = lax.dot_general(
        table_ref[...], kind, (((0,), (0,)), ((), ())), preferred_element_type=F32
    )
    states[1] = (state_ref[...].astype(F32).T + embedded).astype(BF16)
    pl.semaphore_wait(barrier, len(peers) + len(others))
    place_copies, state_copies = [], []
    for i, (device, slot) in enumerate(((left, 2), (right, 0), (far, 3))):
        place_copies.append(
            send(places.at[1], places.at[slot], halo_send.at[i], halo_recv.at[i], {"graph": device})
        )
    for i, (device, slot) in enumerate(((left, 2), (right, 0), (far, 3))):
        state_copies.append(
            send(
                states.at[1], states.at[slot], halo_send.at[3 + i], halo_recv.at[3 + i], {"graph": device}
            )
        )

    w_rad_t[...] = w_rad_ref[...].astype(F32).T.astype(BF16)
    w_src_t[...] = w_src_ref[...].astype(F32).T.astype(BF16)
    w_out_t[...] = jnp.broadcast_to(w_out_ref[...], (channels, LANES)).T
    centre[...] = centers(count)[0]
    spread[...] = jnp.zeros_like(spread)
    incoming[...] = jnp.zeros_like(incoming)
    grad_radial[...] = jnp.zeros_like(grad_radial)
    grad_source[...] = jnp.zeros_like(grad_source)
    grad_out[...] = jnp.zeros_like(grad_out)
    prepare_indices(groups, source_ref, count_ref, lanes, rows_of, pick, tiles)
    for copy in place_copies:
        copy.wait()

    def distances(n, table_rows):
        source_place = pick_three(places, table_rows, lanes[n], rows_of[n])
        delta = [source_place[c] - places[1, pl.ds(8 * c + n, 1), :] for c in range(3)]
        dist = jnp.sqrt(delta[0] * delta[0] + delta[1] * delta[1] + delta[2] * delta[2] + 0.25)
        for c in range(3):
            scalar[n, c * PAD : (c + 1) * PAD] = delta[c] / dist
        scalar[n, 3 * PAD :] = dist

    def bases(n):
        def one(j, unused):
            place = pl.ds(pl.multiple_of(j * LANES, LANES), LANES)
            bump, slant = basis(scalar[n, pl.ds(3 * PAD + j, 1), :], centre[...], gamma)
            bumps[n, :, place] = bump
            slants[n, :, place] = slant
            return unused

        lax.fori_loop(0, DEG, one, 0)

    def before(n, unused):
        distances(n, 21)
        bases(n)
        return unused

    lax.fori_loop(1, tiles, before, 0)
    distances(0, 28)
    bases(0)
    for copy in state_copies:
        copy.wait()
    for half in range(28):
        at = (half % 7) * LANES
        stack[
            (half // 2) * channels : (half // 2 + 1) * channels,
            (half % 2) * LANES : (half % 2 + 1) * LANES,
        ] = states[half // 7, :, at : at + LANES]

    def forward(n, chunks):
        agg_acc[...] = jnp.zeros_like(agg_acc)

        def piece(i, unused):
            place = pl.ds(pl.multiple_of(i * WIDE, WIDE), WIDE)
            numbers = lax.broadcasted_iota(jnp.int32, (256, LANES), 0).astype(F32)
            ones, hi = [], []
            for j in range(STEP):
                column = pick[n, pl.ds(i * STEP + j, 1), :]
                ones.append((numbers == column).astype(BF16))
                hi.append(pick[n, pl.ds(PAD + i * STEP + j, 1), :])
            ones = jnp.concatenate(ones, axis=1)
            hi = jnp.broadcast_to(jnp.concatenate(hi, axis=1), (channels, WIDE))
            onehots[:, place] = ones
            found = jnp.dot(stack[: chunks * channels], ones, preferred_element_type=F32)
            rows = found[:channels]
            for c in range(1, chunks):
                rows = jnp.where(hi == float(c), found[c * channels : (c + 1) * channels], rows)
            rows = rows.astype(BF16)
            rows_keep[n, :, place] = rows
            query = jnp.dot(w_src_t[...], rows, preferred_element_type=F32)
            radial = jnp.dot(w_rad_t[...], bumps[n, :, place], preferred_element_type=F32)
            slope = jnp.dot(w_rad_t[...], slants[n, :, place], preferred_element_type=F32)
            query_keep[n, :, place] = query.astype(BF16)
            slope_keep[n, :, place] = slope.astype(BF16)
            radial_keep[n, :, place] = radial.astype(BF16)
            product[:, place] = query * slope
            term = radial * query
            total = term[:, :LANES]
            for j in range(1, STEP):
                total = total + term[:, j * LANES : (j + 1) * LANES]
            agg_acc[...] += total
            return unused

        lax.fori_loop(0, DEG // STEP, piece, 0)
        agg = 0.2 * agg_acc[...]
        agg_keep[n] = agg
        first, _ = node_terms(agg)
        readout = 0.2 * first * w_out_t[...]
        inward = [jnp.zeros((1, LANES), F32)] * 3
        lhs = []
        chunk = lax.broadcasted_iota(jnp.int32, (16, LANES), 0).astype(F32)
        for j in range(DEG):
            pull = jnp.sum(readout * product[:, j * LANES : (j + 1) * LANES], axis=0, keepdims=True)
            here = chunk == pick[n, PAD + j : PAD + j + 1, :]
            high, low = [], []
            for c in range(3):
                moved = pull * scalar[n, c * PAD + j : c * PAD + j + 1, :]
                inward[c] = inward[c] + moved
                term = jnp.where(here, moved, 0.0)
                top = term.astype(BF16)
                high.append(top)
                low.append((term - top.astype(F32)).astype(BF16))
            lhs.append(jnp.concatenate(high + low, axis=0))
        lhs = jnp.concatenate(lhs, axis=1)
        spread[...] += lax.dot_general(lhs, onehots[...], NT, preferred_element_type=F32)
        for c in range(3):
            incoming[pl.ds(8 * c + n, 1), :] = inward[c]

    lax.fori_loop(1, tiles, lambda n, u: (forward(n, 11), u)[1], 0)
    forward(0, 14)

    outgoing[...] = jnp.zeros_like(outgoing)
    total = spread[:48] + spread[48:]
    for c in range(3):
        for r in range(28):
            at = c * 8 + r % 7
            outgoing[r // 7, at : at + 1, :] = total[
                c * 16 + r // 2 : c * 16 + r // 2 + 1, (r % 2) * LANES : (r % 2 + 1) * LANES
            ]
    copies = []
    for i, (device, slot) in enumerate(((left, 0), (right, 2), (far, 3))):
        copies.append(
            send(outgoing.at[slot], terms.at[i], term_send.at[i], term_recv.at[i], {"graph": device})
        )
    for copy in copies:
        copy.wait()
    forces = incoming[...] - (outgoing[1] + terms[0] + terms[1] + terms[2])
    miss = forces - wanted[...]
    backs[1] = 2.0 * weight_loss * miss
    copies = []
    for i, (device, slot) in enumerate(((left, 2), (right, 0), (far, 3))):
        copies.append(
            send(backs.at[1], backs.at[slot], term_send.at[3 + i], term_recv.at[3 + i], {"graph": device})
        )
    for c in range(3):
        for n in range(tiles):
            forces_ref[c, :, n * LANES : (n + 1) * LANES] = forces[8 * c + n : 8 * c + n + 1, :]
    loss = weight_loss * jnp.sum(miss * miss, axis=(0, 1), keepdims=True)
    for copy in copies:
        copy.wait()

    def backward(n, table_rows):
        source_back = pick_three(backs, table_rows, lanes[n], rows_of[n])
        lam = jnp.zeros((PAD, LANES), F32)
        for c in range(3):
            lam = lam + (backs[1, pl.ds(8 * c + n, 1), :] - source_back[c]) * scalar[
                n, c * PAD : (c + 1) * PAD
            ]
        lam_ref[...] = 0.2 * lam
        first, second = node_terms(agg_keep[n])
        w_out = w_out_t[...]
        readout = first * w_out

        def gather(j, total):
            place = pl.ds(pl.multiple_of(j * LANES, LANES), LANES)
            return total + lam_ref[pl.ds(j, 1), :] * (
                query_keep[n, :, place].astype(F32) * slope_keep[n, :, place].astype(F32)
            )

        dread = lax.fori_loop(0, DEG, gather, jnp.zeros((channels, LANES), F32))
        grad_out[...] += dread * first
        plain = 0.2 * dread * w_out * second

        def piece(j, unused):
            place = pl.ds(pl.multiple_of(j * LANES, LANES), LANES)
            over_slope = lam_ref[pl.ds(j, 1), :] * readout
            query = query_keep[n, :, place].astype(F32)
            plain_coef[:, place] = (plain * query).astype(BF16)
            slope_coef[:, place] = (over_slope * query).astype(BF16)
            wants[:, place] = (
                over_slope * slope_keep[n, :, place].astype(F32)
                + plain * radial_keep[n, :, place].astype(F32)
            ).astype(BF16)
            return unused

        lax.fori_loop(0, DEG, piece, 0)
        grad_radial[...] += lax.dot_general(
            plain_coef[...], bumps[n], NT, preferred_element_type=F32
        ) + lax.dot_general(slope_coef[...], slants[n], NT, preferred_element_type=F32)
        grad_source[...] += lax.dot_general(
            rows_keep[n], wants[...], NT, preferred_element_type=F32
        )

    lax.fori_loop(1, tiles, lambda n, u: (backward(n, 21), u)[1], 0)
    backward(0, 28)

    radial = grad_radial[...].T
    source = grad_source[...]
    for i in range(groups):
        for k in range(3):
            at = (3 * i + k) * 8
            own[i, 8 * k : 8 * k + 8] = (
                radial[at : at + 8] if at < count else source[at - count : at - count + 8]
            )
        own[i, 24:] = jnp.zeros((8, LANES), F32)
    own[0, 24:25] = jnp.sum(grad_out[...].T, axis=0, keepdims=True)
    own[0, 25:26] = jnp.broadcast_to(loss, (1, LANES))
    copies = []
    for i, p in enumerate(peers):
        copies.append(send(own.at[p], pieces.at[i], piece_send.at[i], piece_recv.at[i], {"graph": p}))
    for copy in copies:
        copy.wait()
    total = own[me]
    for i in range(groups - 1):
        total = total + pieces[i]
    part[batch] = total
    copies = []
    for i, b in enumerate(others):
        copies.append(send(part.at[batch], part.at[batch], part_send.at[i], part_recv.at[i], {"dp": b}))
    for copy in copies:
        copy.wait()
    total = part[0]
    for i in range(1, batches):
        total = total + part[i]
    whole[me] = total
    copies = []
    for i, p in enumerate(peers):
        copies.append(send(whole.at[me], whole.at[me], whole_send.at[i], whole_recv.at[i], {"graph": p}))
    for copy in copies:
        copy.wait()
    whole_ref[...] = whole[...]


def output_kernel(whole_ref, from_ref, forces_ref, radial_ref, source_ref, out_ref, loss_ref):
    count = radial_ref.shape[0]
    for i in range(whole_ref.shape[0]):
        for k in range(3):
            at = (3 * i + k) * 8
            if at < count:
                radial_ref[at : at + 8] = whole_ref[i, 8 * k : 8 * k + 8]
            else:
                source_ref[at - count : at - count + 8] = whole_ref[i, 8 * k : 8 * k + 8]
    out_ref[...] = whole_ref[0, 24:25]
    loss_ref[...] = whole_ref[0, 25:26, :1]
    forces_ref[...] = from_ref[...]


def whole_vmem():
    return pl.BlockSpec(memory_space=VMEM)


def local(
    node_state,
    atom_types,
    positions,
    force_ref,
    edge_source,
    edge_count,
    type_table,
    w_rad,
    w_src,
    w_out,
):
    nodes, channels = node_state.shape[1:]
    groups = lax.axis_size("graph")
    batches = lax.axis_size("dp")
    weight_loss = 1.0 / math.sqrt(3.0 * nodes * groups * node_state.shape[0] * batches)
    count = w_rad.shape[0]
    tiles = nodes // LANES
    wide = DEG * LANES
    dma = pltpu.SemaphoreType.DMA

    def shape(*dims, dtype=F32):
        return jax.ShapeDtypeStruct(dims, dtype)

    others = max(batches - 1, 1)
    forces, whole = pl.pallas_call(
        functools.partial(fused_kernel, groups, batches, weight_loss),
        out_shape=(shape(3, 1, nodes), shape(groups, 32, LANES)),
        in_specs=[whole_vmem()] * 10,
        out_specs=(whole_vmem(),) * 2,
        scratch_shapes=[
            VMEM((4, channels, nodes), BF16),
            VMEM((4, PAD, LANES), F32),
            VMEM((14 * channels, 256), BF16),
            VMEM((channels, count), BF16),
            VMEM((channels, channels), BF16),
            VMEM((channels, LANES), F32),
            VMEM((count, LANES), F32),
            VMEM((tiles, PAD, LANES), jnp.int32),
            VMEM((tiles, PAD, LANES), jnp.int32),
            VMEM((tiles, 2 * PAD, LANES), F32),
            VMEM((tiles, 4 * PAD, LANES), F32),
            VMEM((tiles, count, wide), BF16),
            VMEM((tiles, count, wide), BF16),
            VMEM((tiles, channels, wide), BF16),
            VMEM((tiles, channels, wide), BF16),
            VMEM((tiles, channels, wide), BF16),
            VMEM((tiles, channels, wide), BF16),
            VMEM((tiles, channels, LANES), F32),
            VMEM((256, wide), BF16),
            VMEM((channels, wide), F32),
            VMEM((channels, LANES), F32),
            VMEM((96, 256), F32),
            VMEM((PAD, LANES), F32),
            VMEM((4, PAD, LANES), F32),
            VMEM((3, PAD, LANES), F32),
            VMEM((PAD, LANES), F32),
            VMEM((4, PAD, LANES), F32),
            VMEM((PAD, LANES), F32),
            VMEM((channels, wide), BF16),
            VMEM((channels, wide), BF16),
            VMEM((channels, wide), BF16),
            VMEM((channels, count), F32),
            VMEM((channels, channels), F32),
            VMEM((channels, LANES), F32),
            VMEM((groups, 32, LANES), F32),
            VMEM((groups - 1, 32, LANES), F32),
            VMEM((batches, 32, LANES), F32),
            VMEM((groups, 32, LANES), F32),
            dma((6,)),
            dma((6,)),
            dma((6,)),
            dma((6,)),
            dma((groups - 1,)),
            dma((groups - 1,)),
            dma((others,)),
            dma((others,)),
            dma((groups - 1,)),
            dma((groups - 1,)),
        ],
        compiler_params=pltpu.CompilerParams(
            collective_id=0, has_side_effects=True, vmem_limit_bytes=LIMIT
        ),
        name="fused",
    )(
        node_state[0],
        atom_types,
        positions.transpose(1, 0, 2),
        force_ref.transpose(1, 0, 2),
        edge_source,
        edge_count,
        type_table,
        w_rad,
        w_src,
        w_out.reshape(1, channels),
    )
    forces, grad_radial, grad_source, grad_out, loss = pl.pallas_call(
        output_kernel,
        out_shape=(
            shape(3, 1, nodes),
            shape(count, channels),
            shape(channels, channels),
            shape(1, channels),
            shape(1, 1),
        ),
        in_specs=[whole_vmem()] * 2,
        out_specs=(whole_vmem(),) * 5,
        name="output",
    )(whole, forces)
    return forces.transpose(1, 0, 2), grad_radial, grad_source, grad_out[0], loss[0, 0]


def solution(mesh):
    in_specs = (
        P("dp", "graph", None),
        P("dp", "graph"),
        P("dp", None, "graph"),
        P("dp", None, "graph"),
        P("dp", "graph"),
        P("dp", "graph"),
        P(),
        P(),
        P(),
        P(),
    )
    out_specs = (P("dp", None, "graph"), P(), P(), P(), P())
    return jax.shard_map(local, mesh=mesh, in_specs=in_specs, out_specs=out_specs, check_vma=False)
```

time: 891 us -> 96.4 us (0.11)
  matrix products: 434 us -> 0 us
  local copies, waits for them, and re-layouts: 144 us -> 0 us
  waiting for transfers between devices: 140 us -> 0 us
  blocking collectives: 110 us -> 0 us
  Pallas kernels: 0 us -> 94.9 us
  other arithmetic: 37.5 us -> 0 us
  between operations: 15.9 us -> 1.29 us
    dot_general x37 -> x0, matrix products: 434 us -> none  [the longest x20 230 us: one_block(): lax.dot_general(table, select, (((1,), (1,)), ((), ())), precision=lax.Pr...]
    pallas_call x0 -> x2, Pallas kernels: none -> 94.9 us  [the longest x1 93.3 us: local(): pl.pallas_call(functools.partial(fused_kernel, groups, batches, weight_lo...]
    psum x1 -> x0, waiting for transfers between devices: 74.9 us -> none  [local(): lax.psum((stacked, grad_out_part, loss_part), ('dp', 'graph'))]
    psum x1 -> x0, blocking collectives: 66 us -> none  [local(): lax.psum((stacked, grad_out_part, loss_part), ('dp', 'graph'))]
    unnamed x4 -> x0, waiting for transfers between devices: 65.3 us -> none
    reshape x6 -> x0, local copies, waits for them, and re-layouts: 46.5 us -> none  [the longest x2 21.9 us: widen_rows(): jnp.broadcast_to(values[:, None, :], (nodes, degree, values.shape[1]))]
    all_gather x2 -> x0, blocking collectives: 44.2 us -> none  [the longest x1 23.1 us: local(): gathered_place = lax.all_gather(places, 'graph', axis=1, tiled=True)]
    gather x1 -> x0, local copies, waits for them, and re-layouts: 36.7 us -> none  [local(): source_rows = jnp.take(every_state, picked, axis=0)]
  transfers between devices with their start and end apart: 3 -> 0, of which waited for: 2 -> 0; matrix products, arithmetic and copies ran while one was open for 16% -> 0% of each run, Pallas kernels for 0% -> 0%
where the time goes in v2:
time: 96.4 us; the launch traced here: 96.2 us
  Pallas kernels  94.9 us (98%)
  between operations  1.29 us (1%)
    pallas_call x1, Pallas kernels, local(): pl.pallas_call(functools.partial(fused_kernel, groups, batches, weight_lo...  93.3 us

profile of v2, /device:TPU:1, one launch (start us, length us, event | category | flops | bytes accessed | tf_op | source)
XLA Modules:
  0.0 96.2 jit_solution(13679698821478459346)
XLA Ops:
  1.3 93.3 %fused.1 = (f32[3,1,896]{2,1,0:T(1,128)}, f32[16,32,128]{2,1,0:T(8,128)}) custom-call(bf16[896,128]{1,0:T(8,128)(2,1)} %bitcast.7, s32[1,896]{1,0:T(1,128)} %types_ref.1, f32[3,1,896]{2,1,0:T(1,128)} %bitcast.8, f32[3,1,896]{2,1,0:T(1,128)} %bitcast.9, s32[1,17920]{1,0:T(1,128)} %source_ref.1, s32[1,1]{1,0:T(1,128)S(6)} %copy.15.count_ref, ...), custom_call_target="tpu_custom_call" | custom-call | tf_op jit(solution)/shard_map/fused/pallas_call | solution.py:486
  94.6 1.6 %output.1 = (f32[3,1,896]{2,1,0:T(1,128)}, f32[256,128]{1,0:T(8,128)}, f32[128,128]{1,0:T(8,128)}, f32[1,128]{1,0:T(1,128)}, f32[1,1]{1,0:T(1,128)}) custom-call(f32[16,32,128]{2,1,0:T(8,128)} %get-tuple-element.12.whole_ref, f32[3,1,896]{2,1,0:T(1,128)} %get-tuple-element.13.from_ref), custom_call_target="tpu_custom_call" | custom-call | tf_op jit(solution)/shard_map/output/pallas_call | solution.py:557

commit v3 on v2

--- a/solution.py
+++ b/solution.py
@@ -17,8 +17,7 @@
 LANES = 128
 VMEM = pltpu.VMEM
 LIMIT = 60 * 1024 * 1024
-STEP = 10
-WIDE = STEP * LANES
+WIDE = DEG * LANES
 
 
 def partners(groups):
@@ -146,19 +145,22 @@
     slope_keep,
     radial_keep,
     agg_keep,
-    onehots,
-    product,
-    agg_acc,
+    onehots_a,
+    onehots_b,
+    product_a,
+    product_b,
     spread,
     incoming,
     outgoing,
     terms,
     wanted,
     backs,
-    lam_ref,
-    plain_coef,
-    slope_coef,
-    wants,
+    plain_a,
+    slope_a,
+    wants_a,
+    plain_b,
+    slope_b,
+    wants_b,
     grad_radial,
     grad_source,
     grad_out,
@@ -266,54 +268,45 @@
             (half % 2) * LANES : (half % 2 + 1) * LANES,
         ] = states[half // 7, :, at : at + LANES]
 
-    def forward(n, chunks):
-        agg_acc[...] = jnp.zeros_like(agg_acc)
-
-        def piece(i, unused):
-            place = pl.ds(pl.multiple_of(i * WIDE, WIDE), WIDE)
-            numbers = lax.broadcasted_iota(jnp.int32, (256, LANES), 0).astype(F32)
-            ones, hi = [], []
-            for j in range(STEP):
-                column = pick[n, pl.ds(i * STEP + j, 1), :]
-                ones.append((numbers == column).astype(BF16))
-                hi.append(pick[n, pl.ds(PAD + i * STEP + j, 1), :])
-            ones = jnp.concatenate(ones, axis=1)
-            hi = jnp.broadcast_to(jnp.concatenate(hi, axis=1), (channels, WIDE))
-            onehots[:, place] = ones
-            found = jnp.dot(stack[: chunks * channels], ones, preferred_element_type=F32)
-            rows = found[:channels]
-            for c in range(1, chunks):
-                rows = jnp.where(hi == float(c), found[c * channels : (c + 1) * channels], rows)
-            rows = rows.astype(BF16)
-            rows_keep[n, :, place] = rows
-            query = jnp.dot(w_src_t[...], rows, preferred_element_type=F32)
-            radial = jnp.dot(w_rad_t[...], bumps[n, :, place], preferred_element_type=F32)
-            slope = jnp.dot(w_rad_t[...], slants[n, :, place], preferred_element_type=F32)
-            query_keep[n, :, place] = query.astype(BF16)
-            slope_keep[n, :, place] = slope.astype(BF16)
-            radial_keep[n, :, place] = radial.astype(BF16)
-            product[:, place] = query * slope
-            term = radial * query
-            total = term[:, :LANES]
-            for j in range(1, STEP):
-                total = total + term[:, j * LANES : (j + 1) * LANES]
-            agg_acc[...] += total
-            return unused
-
-        lax.fori_loop(0, DEG // STEP, piece, 0)
-        agg = 0.2 * agg_acc[...]
-        agg_keep[n] = agg
-        first, _ = node_terms(agg)
+    def gather(n, chunks, onehots, product):
+        numbers = lax.broadcasted_iota(jnp.int32, (256, LANES), 0).astype(F32)
+        ones = jnp.concatenate(
+            [(numbers == pick[n, pl.ds(j, 1), :]).astype(BF16) for j in range(DEG)], axis=1
+        )
+        hi = jnp.concatenate([pick[n, pl.ds(PAD + j, 1), :] for j in range(DEG)], axis=1)
+        hi = jnp.broadcast_to(hi, (channels, WIDE))
+        found = jnp.dot(stack[: chunks * channels], ones, preferred_element_type=F32)
+        onehots[...] = ones
+        rows = found[:channels]
+        for c in range(1, chunks):
+            rows = jnp.where(hi == float(c), found[c * channels : (c + 1) * channels], rows)
+        rows = rows.astype(BF16)
+        rows_keep[n] = rows
+        query = jnp.dot(w_src_t[...], rows, preferred_element_type=F32)
+        radial = jnp.dot(w_rad_t[...], bumps[n], preferred_element_type=F32)
+        slope = jnp.dot(w_rad_t[...], slants[n], preferred_element_type=F32)
+        query_keep[n] = query.astype(BF16)
+        slope_keep[n] = slope.astype(BF16)
+        radial_keep[n] = radial.astype(BF16)
+        product[...] = query * slope
+        term = radial * query
+        total = term[:, :LANES]
+        for j in range(1, DEG):
+            total = total + term[:, j * LANES : (j + 1) * LANES]
+        agg_keep[n] = 0.2 * total
+
+    def pull(n, onehots, product):
+        first, _ = node_terms(agg_keep[n])
         readout = 0.2 * first * w_out_t[...]
         inward = [jnp.zeros((1, LANES), F32)] * 3
         lhs = []
         chunk = lax.broadcasted_iota(jnp.int32, (16, LANES), 0).astype(F32)
         for j in range(DEG):
-            pull = jnp.sum(readout * product[:, j * LANES : (j + 1) * LANES], axis=0, keepdims=True)
+            force = jnp.sum(readout * product[:, j * LANES : (j + 1) * LANES], axis=0, keepdims=True)
             here = chunk == pick[n, PAD + j : PAD + j + 1, :]
             high, low = [], []
             for c in range(3):
-                moved = pull * scalar[n, c * PAD + j : c * PAD + j + 1, :]
+                moved = force * scalar[n, c * PAD + j : c * PAD + j + 1, :]
                 inward[c] = inward[c] + moved
                 term = jnp.where(here, moved, 0.0)
                 top = term.astype(BF16)
@@ -325,8 +318,22 @@
         for c in range(3):
             incoming[pl.ds(8 * c + n, 1), :] = inward[c]
 
-    lax.fori_loop(1, tiles, lambda n, u: (forward(n, 11), u)[1], 0)
-    forward(0, 14)
+    agg_keep[0] = jnp.zeros((channels, LANES), F32)
+    product_b[...] = jnp.zeros_like(product_b)
+    onehots_b[...] = jnp.zeros_like(onehots_b)
+
+    def two_forward(i, unused):
+        n = 2 * i + 1
+        pull(n - 1, onehots_b, product_b)
+        gather(n, 11, onehots_a, product_a)
+        pull(n, onehots_a, product_a)
+        gather(n + 1, 11, onehots_b, product_b)
+        return unused
+
+    lax.fori_loop(0, (tiles - 1) // 2, two_forward, 0)
+    pull(tiles - 1, onehots_b, product_b)
+    gather(0, 14, onehots_a, product_a)
+    pull(0, onehots_a, product_a)
 
     outgoing[...] = jnp.zeros_like(outgoing)
     total = spread[:48] + spread[48:]
@@ -358,41 +365,37 @@
     for copy in copies:
         copy.wait()
 
-    def backward(n, table_rows):
+    def coefficients(n, table_rows, plain_coef, slope_coef, wants):
         source_back = pick_three(backs, table_rows, lanes[n], rows_of[n])
         lam = jnp.zeros((PAD, LANES), F32)
         for c in range(3):
             lam = lam + (backs[1, pl.ds(8 * c + n, 1), :] - source_back[c]) * scalar[
                 n, c * PAD : (c + 1) * PAD
             ]
-        lam_ref[...] = 0.2 * lam
+        lam = 0.2 * lam
         first, second = node_terms(agg_keep[n])
         w_out = w_out_t[...]
         readout = first * w_out
-
-        def gather(j, total):
-            place = pl.ds(pl.multiple_of(j * LANES, LANES), LANES)
-            return total + lam_ref[pl.ds(j, 1), :] * (
-                query_keep[n, :, place].astype(F32) * slope_keep[n, :, place].astype(F32)
+        dread = jnp.zeros((channels, LANES), F32)
+        for j in range(DEG):
+            at = slice(j * LANES, (j + 1) * LANES)
+            dread = dread + lam[j : j + 1] * (
+                query_keep[n, :, at].astype(F32) * slope_keep[n, :, at].astype(F32)
             )
-
-        dread = lax.fori_loop(0, DEG, gather, jnp.zeros((channels, LANES), F32))
         grad_out[...] += dread * first
         plain = 0.2 * dread * w_out * second
-
-        def piece(j, unused):
-            place = pl.ds(pl.multiple_of(j * LANES, LANES), LANES)
-            over_slope = lam_ref[pl.ds(j, 1), :] * readout
-            query = query_keep[n, :, place].astype(F32)
-            plain_coef[:, place] = (plain * query).astype(BF16)
-            slope_coef[:, place] = (over_slope * query).astype(BF16)
-            wants[:, place] = (
-                over_slope * slope_keep[n, :, place].astype(F32)
-                + plain * radial_keep[n, :, place].astype(F32)
+        for j in range(DEG):
+            at = slice(j * LANES, (j + 1) * LANES)
+            over_slope = lam[j : j + 1] * readout
+            query = query_keep[n, :, at].astype(F32)
+            plain_coef[:, at] = (plain * query).astype(BF16)
+            slope_coef[:, at] = (over_slope * query).astype(BF16)
+            wants[:, at] = (
+                over_slope * slope_keep[n, :, at].astype(F32)
+                + plain * radial_keep[n, :, at].astype(F32)
             ).astype(BF16)
-            return unused
-
-        lax.fori_loop(0, DEG, piece, 0)
+
+    def products(n, plain_coef, slope_coef, wants):
         grad_radial[...] += lax.dot_general(
             plain_coef[...], bumps[n], NT, preferred_element_type=F32
         ) + lax.dot_general(slope_coef[...], slants[n], NT, preferred_element_type=F32)
@@ -400,8 +403,23 @@
             rows_keep[n], wants[...], NT, preferred_element_type=F32
         )
 
-    lax.fori_loop(1, tiles, lambda n, u: (backward(n, 21), u)[1], 0)
-    backward(0, 28)
+    coef_a = (plain_a, slope_a, wants_a)
+    coef_b = (plain_b, slope_b, wants_b)
+    for ref in coef_b:
+        ref[...] = jnp.zeros_like(ref)
+
+    def two_backward(i, unused):
+        n = 2 * i + 1
+        products(n - 1, *coef_b)
+        coefficients(n, 21, *coef_a)
+        products(n, *coef_a)
+        coefficients(n + 1, 21, *coef_b)
+        return unused
+
+    lax.fori_loop(0, (tiles - 1) // 2, two_backward, 0)
+    products(tiles - 1, *coef_b)
+    coefficients(0, 28, *coef_a)
+    products(0, *coef_a)
 
     radial = grad_radial[...].T
     source = grad_source[...]
@@ -507,19 +525,15 @@
             VMEM((tiles, channels, wide), BF16),
             VMEM((tiles, channels, wide), BF16),
             VMEM((tiles, channels, LANES), F32),
-            VMEM((256, wide), BF16),
-            VMEM((channels, wide), F32),
-            VMEM((channels, LANES), F32),
+            *[VMEM((256, wide), BF16)] * 2,
+            *[VMEM((channels, wide), F32)] * 2,
             VMEM((96, 256), F32),
             VMEM((PAD, LANES), F32),
             VMEM((4, PAD, LANES), F32),
             VMEM((3, PAD, LANES), F32),
             VMEM((PAD, LANES), F32),
             VMEM((4, PAD, LANES), F32),
-            VMEM((PAD, LANES), F32),
-            VMEM((channels, wide), BF16),
-            VMEM((channels, wide), BF16),
-            VMEM((channels, wide), BF16),
+            *[VMEM((channels, wide), BF16)] * 6,
             VMEM((channels, count), F32),
             VMEM((channels, channels), F32),
             VMEM((channels, LANES), F32),

time: 96.4 us -> 80.4 us (0.83)
  Pallas kernels: 94.9 us -> 78.9 us
    pallas_call x1, Pallas kernels: 93.3 us -> 77.3 us  [local(): pl.pallas_call(functools.partial(fused_kernel, groups, batches, weight_lo...]
where the time goes in v3:
time: 80.4 us; the launch traced here: 80.2 us
  Pallas kernels  78.9 us (98%)
  between operations  1.29 us (2%)
    pallas_call x1, Pallas kernels, local(): pl.pallas_call(functools.partial(fused_kernel, groups, batches, weight_lo...  77.3 us
    pallas_call x1, Pallas kernels, local(): pl.pallas_call(output_kernel, out_shape=(shape(3, 1, nodes), shape(count,...  1.64 us

profile of v3, /device:TPU:1, one launch (start us, length us, event | category | flops | bytes accessed | tf_op | source)
XLA Modules:
  0.0 80.2 jit_solution(14095426776712048540)
XLA Ops:
  1.3 77.3 %fused.1 = (f32[3,1,896]{2,1,0:T(1,128)}, f32[16,32,128]{2,1,0:T(8,128)}) custom-call(bf16[896,128]{1,0:T(8,128)(2,1)} %bitcast.7, s32[1,896]{1,0:T(1,128)} %types_ref.1, f32[3,1,896]{2,1,0:T(1,128)} %bitcast.8, f32[3,1,896]{2,1,0:T(1,128)} %bitcast.9, s32[1,17920]{1,0:T(1,128)} %source_ref.1, s32[1,1]{1,0:T(1,128)S(6)} %copy.15.count_ref, ...), custom_call_target="tpu_custom_call" | custom-call | tf_op jit(solution)/shard_map/fused/pallas_call | solution.py:504
  78.6 1.6 %output.1 = (f32[3,1,896]{2,1,0:T(1,128)}, f32[256,128]{1,0:T(8,128)}, f32[128,128]{1,0:T(8,128)}, f32[1,128]{1,0:T(1,128)}, f32[1,1]{1,0:T(1,128)}) custom-call(f32[16,32,128]{2,1,0:T(8,128)} %get-tuple-element.12.whole_ref, f32[3,1,896]{2,1,0:T(1,128)} %get-tuple-element.13.from_ref), custom_call_target="tpu_custom_call" | custom-call | tf_op jit(solution)/shard_map/output/pallas_call | solution.py:571

commit v4 on v3

--- a/solution.py
+++ b/solution.py
@@ -16,8 +16,9 @@
 PAD = 24
 LANES = 128
 VMEM = pltpu.VMEM
-LIMIT = 60 * 1024 * 1024
+LIMIT = 62 * 1024 * 1024
 WIDE = DEG * LANES
+NEAR = 16
 
 
 def partners(groups):
@@ -85,7 +86,9 @@
     return first, second
 
 
-def prepare_indices(groups, source_ref, count_ref, lanes_ref, rows_ref, pick_ref, tiles):
+def prepare_indices(
+    groups, source_ref, count_ref, lanes_ref, rows_ref, pick_ref, compact_ref, tiles
+):
     me = lax.axis_index("graph")
     slot = lax.broadcasted_iota(jnp.int32, (PAD, LANES), 1) * DEG + lax.broadcasted_iota(
         jnp.int32, (PAD, LANES), 0
@@ -109,6 +112,17 @@
         rows_ref[n] = picked >> 7
         pick_ref[n, :PAD] = jnp.where(live, (picked & 255).astype(F32), -1.0)
         pick_ref[n, PAD:] = (picked >> 8).astype(F32)
+    lane = lax.broadcasted_iota(jnp.int32, (8, LANES), 1)
+    here = (lane >> 4) == lax.broadcasted_iota(jnp.int32, (8, LANES), 0)
+    for g in range(2):
+        for r in range(PAD // 8):
+            values = pick_ref[0, g * PAD + 8 * r : g * PAD + 8 * r + 8]
+            values = jnp.take_along_axis(
+                values, LANES - NEAR + (lane & (NEAR - 1)), axis=1, mode="promise_in_bounds"
+            )
+            compact_ref[8 * g + r : 8 * g + r + 1] = jnp.sum(
+                jnp.where(here, values, 0.0), axis=0, keepdims=True
+            )
 
 
 def fused_kernel(
@@ -137,9 +151,10 @@
     lanes,
     rows_of,
     pick,
+    compact,
     scalar,
-    bumps,
-    slants,
+    basis_a,
+    basis_b,
     rows_keep,
     query_keep,
     slope_keep,
@@ -155,11 +170,7 @@
     terms,
     wanted,
     backs,
-    plain_a,
-    slope_a,
     wants_a,
-    plain_b,
-    slope_b,
     wants_b,
     grad_radial,
     grad_source,
@@ -207,13 +218,15 @@
         table_ref[...], kind, (((0,), (0,)), ((), ())), preferred_element_type=F32
     )
     states[1] = (state_ref[...].astype(F32).T + embedded).astype(BF16)
+    prepare_indices(groups, source_ref, count_ref, lanes, rows_of, pick, compact, tiles)
     pl.semaphore_wait(barrier, len(peers) + len(others))
     place_copies, state_copies = [], []
-    for i, (device, slot) in enumerate(((left, 2), (right, 0), (far, 3))):
+    targets = ((left, 2), (right, 0), (far, 3))
+    for i, (device, slot) in enumerate(targets):
         place_copies.append(
             send(places.at[1], places.at[slot], halo_send.at[i], halo_recv.at[i], {"graph": device})
         )
-    for i, (device, slot) in enumerate(((left, 2), (right, 0), (far, 3))):
+    for i, (device, slot) in enumerate(targets):
         state_copies.append(
             send(
                 states.at[1], states.at[slot], halo_send.at[3 + i], halo_recv.at[3 + i], {"graph": device}
@@ -229,7 +242,6 @@
     grad_radial[...] = jnp.zeros_like(grad_radial)
     grad_source[...] = jnp.zeros_like(grad_source)
     grad_out[...] = jnp.zeros_like(grad_out)
-    prepare_indices(groups, source_ref, count_ref, lanes, rows_of, pick, tiles)
     for copy in place_copies:
         copy.wait()
 
@@ -241,50 +253,77 @@
             scalar[n, c * PAD : (c + 1) * PAD] = delta[c] / dist
         scalar[n, 3 * PAD :] = dist
 
-    def bases(n):
-        def one(j, unused):
-            place = pl.ds(pl.multiple_of(j * LANES, LANES), LANES)
-            bump, slant = basis(scalar[n, pl.ds(3 * PAD + j, 1), :], centre[...], gamma)
-            bumps[n, :, place] = bump
-            slants[n, :, place] = slant
-            return unused
-
-        lax.fori_loop(0, DEG, one, 0)
-
-    def before(n, unused):
-        distances(n, 21)
-        bases(n)
-        return unused
-
-    lax.fori_loop(1, tiles, before, 0)
+    def bases(n, kept):
+        for j in range(DEG):
+            at = slice(j * LANES, (j + 1) * LANES)
+            bump, slant = basis(scalar[n, 3 * PAD + j : 3 * PAD + j + 1, :], centre[...], gamma)
+            kept[0, :, at] = bump
+            kept[1, :, at] = slant
+
+    def stack_up(halves):
+        for half in halves:
+            at = (half % 7) * LANES
+            stack[
+                (half // 2) * channels : (half // 2 + 1) * channels,
+                (half % 2) * LANES : (half % 2 + 1) * LANES,
+            ] = states[half // 7, :, at : at + LANES]
+
+    lax.fori_loop(1, tiles, lambda n, u: (distances(n, 21), u)[1], 0)
     distances(0, 28)
-    bases(0)
-    for copy in state_copies:
+    def ahead(i, u):
+        bases(2 * i + 1, basis_a.at[i])
+        bases(2 * i + 2, basis_b.at[i])
+        return u
+
+    lax.fori_loop(0, tiles // 2, ahead, 0)
+    bases(0, basis_a.at[3])
+    stack[10 * channels : 11 * channels, LANES:] = jnp.zeros((channels, LANES), BF16)
+    for copy in state_copies[:2]:
         copy.wait()
-    for half in range(28):
-        at = (half % 7) * LANES
-        stack[
-            (half // 2) * channels : (half // 2 + 1) * channels,
-            (half % 2) * LANES : (half % 2 + 1) * LANES,
-        ] = states[half // 7, :, at : at + LANES]
-
-    def gather(n, chunks, onehots, product):
-        numbers = lax.broadcasted_iota(jnp.int32, (256, LANES), 0).astype(F32)
-        ones = jnp.concatenate(
-            [(numbers == pick[n, pl.ds(j, 1), :]).astype(BF16) for j in range(DEG)], axis=1
+    stack_up(range(21))
+
+    numbers = lax.broadcasted_iota(jnp.int32, (256, LANES), 0).astype(F32)
+
+    def look_up(columns, chosen, first, last):
+        ones = jnp.concatenate([(numbers == column).astype(BF16) for column in columns], axis=1)
+        hi = jnp.concatenate(chosen, axis=1)
+        hi = jnp.broadcast_to(hi, (channels, hi.shape[1]))
+        found = jnp.dot(
+            stack[first * channels : last * channels], ones, preferred_element_type=F32
         )
-        hi = jnp.concatenate([pick[n, pl.ds(PAD + j, 1), :] for j in range(DEG)], axis=1)
-        hi = jnp.broadcast_to(hi, (channels, WIDE))
-        found = jnp.dot(stack[: chunks * channels], ones, preferred_element_type=F32)
+        rows = found[:channels]
+        for c in range(1, last - first):
+            rows = jnp.where(
+                hi == float(first + c), found[c * channels : (c + 1) * channels], rows
+            )
+        return ones, rows
+
+    def gather(n, kept, onehots, product):
+        columns = [pick[n, pl.ds(j, 1), :] for j in range(DEG)]
+        chosen = [pick[n, pl.ds(PAD + j, 1), :] for j in range(DEG)]
+        if isinstance(n, int):
+            ones, rows = look_up(columns, chosen, 10, 14)
+            _, near = look_up(
+                [compact[r : r + 1] for r in range(3)], [compact[8 + r : 9 + r] for r in range(3)], 0, 11
+            )
+            last = lax.broadcasted_iota(jnp.int32, (channels, LANES), 1) >= LANES - NEAR
+            parts = []
+            for j in range(DEG):
+                moved = pltpu.roll(
+                    near[:, (j // 8) * LANES : (j // 8 + 1) * LANES],
+                    LANES - NEAR - NEAR * (j % 8),
+                    1,
+                )
+                parts.append(jnp.where(last, moved, rows[:, j * LANES : (j + 1) * LANES]))
+            rows = jnp.concatenate(parts, axis=1)
+        else:
+            ones, rows = look_up(columns, chosen, 0, 11)
         onehots[...] = ones
-        rows = found[:channels]
-        for c in range(1, chunks):
-            rows = jnp.where(hi == float(c), found[c * channels : (c + 1) * channels], rows)
         rows = rows.astype(BF16)
         rows_keep[n] = rows
         query = jnp.dot(w_src_t[...], rows, preferred_element_type=F32)
-        radial = jnp.dot(w_rad_t[...], bumps[n], preferred_element_type=F32)
-        slope = jnp.dot(w_rad_t[...], slants[n], preferred_element_type=F32)
+        radial = jnp.dot(w_rad_t[...], kept[0], preferred_element_type=F32)
+        slope = jnp.dot(w_rad_t[...], kept[1], preferred_element_type=F32)
         query_keep[n] = query.astype(BF16)
         slope_keep[n] = slope.astype(BF16)
         radial_keep[n] = radial.astype(BF16)
@@ -325,14 +364,16 @@
     def two_forward(i, unused):
         n = 2 * i + 1
         pull(n - 1, onehots_b, product_b)
-        gather(n, 11, onehots_a, product_a)
+        gather(n, basis_a.at[i], onehots_a, product_a)
         pull(n, onehots_a, product_a)
-        gather(n + 1, 11, onehots_b, product_b)
+        gather(n + 1, basis_b.at[i], onehots_b, product_b)
         return unused
 
     lax.fori_loop(0, (tiles - 1) // 2, two_forward, 0)
+    state_copies[2].wait()
+    stack_up(range(21, 28))
     pull(tiles - 1, onehots_b, product_b)
-    gather(0, 14, onehots_a, product_a)
+    gather(0, basis_a.at[tiles // 2], onehots_a, product_a)
     pull(0, onehots_a, product_a)
 
     outgoing[...] = jnp.zeros_like(outgoing)
@@ -395,31 +436,31 @@
                 + plain * radial_keep[n, :, at].astype(F32)
             ).astype(BF16)
 
-    def products(n, plain_coef, slope_coef, wants):
+    def products(n, kept, plain_coef, slope_coef, wants):
         grad_radial[...] += lax.dot_general(
-            plain_coef[...], bumps[n], NT, preferred_element_type=F32
-        ) + lax.dot_general(slope_coef[...], slants[n], NT, preferred_element_type=F32)
+            plain_coef[...], kept[0], NT, preferred_element_type=F32
+        ) + lax.dot_general(slope_coef[...], kept[1], NT, preferred_element_type=F32)
         grad_source[...] += lax.dot_general(
             rows_keep[n], wants[...], NT, preferred_element_type=F32
         )
 
-    coef_a = (plain_a, slope_a, wants_a)
-    coef_b = (plain_b, slope_b, wants_b)
+    coef_a = (onehots_a.at[:channels], onehots_a.at[channels : 2 * channels], wants_a)
+    coef_b = (onehots_b.at[:channels], onehots_b.at[channels : 2 * channels], wants_b)
     for ref in coef_b:
         ref[...] = jnp.zeros_like(ref)
 
     def two_backward(i, unused):
         n = 2 * i + 1
-        products(n - 1, *coef_b)
+        products(n - 1, basis_b.at[lax.max(i - 1, 0)], *coef_b)
         coefficients(n, 21, *coef_a)
-        products(n, *coef_a)
+        products(n, basis_a.at[i], *coef_a)
         coefficients(n + 1, 21, *coef_b)
         return unused
 
     lax.fori_loop(0, (tiles - 1) // 2, two_backward, 0)
-    products(tiles - 1, *coef_b)
+    products(tiles - 1, basis_b.at[tiles // 2 - 1], *coef_b)
     coefficients(0, 28, *coef_a)
-    products(0, *coef_a)
+    products(0, basis_a.at[tiles // 2], *coef_a)
 
     radial = grad_radial[...].T
     source = grad_source[...]
@@ -517,9 +558,10 @@
             VMEM((tiles, PAD, LANES), jnp.int32),
             VMEM((tiles, PAD, LANES), jnp.int32),
             VMEM((tiles, 2 * PAD, LANES), F32),
+            VMEM((16, LANES), F32),
             VMEM((tiles, 4 * PAD, LANES), F32),
-            VMEM((tiles, count, wide), BF16),
-            VMEM((tiles, count, wide), BF16),
+            VMEM((tiles // 2 + 1, 2, count, wide), BF16),
+            VMEM((tiles // 2, 2, count, wide), BF16),
             VMEM((tiles, channels, wide), BF16),
             VMEM((tiles, channels, wide), BF16),
             VMEM((tiles, channels, wide), BF16),
@@ -533,7 +575,7 @@
             VMEM((3, PAD, LANES), F32),
             VMEM((PAD, LANES), F32),
             VMEM((4, PAD, LANES), F32),
-            *[VMEM((channels, wide), BF16)] * 6,
+            *[VMEM((channels, wide), BF16)] * 2,
             VMEM((channels, count), F32),
             VMEM((channels, channels), F32),
             VMEM((channels, LANES), F32),

time: 80.4 us -> 78.4 us (0.975)
  Pallas kernels: 78.9 us -> 76.9 us
    pallas_call x1, Pallas kernels: 77.3 us -> 75.3 us  [local(): pl.pallas_call(functools.partial(fused_kernel, groups, batches, weight_lo...]
where the time goes in v4:
time: 78.4 us; the launch traced here: 78.2 us
  Pallas kernels  76.9 us (98%)
  between operations  1.29 us (2%)
    pallas_call x1, Pallas kernels, local(): pl.pallas_call(functools.partial(fused_kernel, groups, batches, weight_lo...  75.3 us
    pallas_call x1, Pallas kernels, local(): pl.pallas_call(output_kernel, out_shape=(shape(3, 1, nodes), shape(count,...  1.64 us

profile of v4, /device:TPU:1, one launch (start us, length us, event | category | flops | bytes accessed | tf_op | source)
XLA Modules:
  0.0 78.2 jit_solution(3470805160665098581)
XLA Ops:
  1.3 75.3 %fused.1 = (f32[3,1,896]{2,1,0:T(1,128)}, f32[16,32,128]{2,1,0:T(8,128)}) custom-call(bf16[896,128]{1,0:T(8,128)(2,1)} %bitcast.7, s32[1,896]{1,0:T(1,128)} %types_ref.1, f32[3,1,896]{2,1,0:T(1,128)} %bitcast.8, f32[3,1,896]{2,1,0:T(1,128)} %bitcast.9, s32[1,17920]{1,0:T(1,128)} %source_ref.1, s32[1,1]{1,0:T(1,128)S(6)} %copy.15.count_ref, ...), custom_call_target="tpu_custom_call" | custom-call | tf_op jit(solution)/shard_map/fused/pallas_call | solution.py:545
  76.6 1.6 %output.1 = (f32[3,1,896]{2,1,0:T(1,128)}, f32[256,128]{1,0:T(8,128)}, f32[128,128]{1,0:T(8,128)}, f32[1,128]{1,0:T(1,128)}, f32[1,1]{1,0:T(1,128)}) custom-call(f32[16,32,128]{2,1,0:T(8,128)} %get-tuple-element.12.whole_ref, f32[3,1,896]{2,1,0:T(1,128)} %get-tuple-element.13.from_ref), custom_call_target="tpu_custom_call" | custom-call | tf_op jit(solution)/shard_map/output/pallas_call | solution.py:613

commit v5 on v4

--- a/solution.py
+++ b/solution.py
@@ -56,20 +56,24 @@
 
 
 def pick_three(tab_ref, rows, lane, row_of):
-    result = [jnp.zeros(lane.shape, F32)] * 3
-    for r in range(rows):
-        here = row_of == r
-        for c in range(3):
-            at = c * 8 + r % 7
-            result[c] = jnp.where(
-                here, lane_pick(tab_ref[r // 7, at : at + 1, :], lane), result[c]
-            )
-    return result
+    results = []
+    for g in range(0, lane.shape[0], 8):
+        lanes_here, row_here = lane[g : g + 8], row_of[g : g + 8]
+        result = [jnp.zeros(lanes_here.shape, F32)] * 3
+        for r in range(rows):
+            here = row_here == r
+            for c in range(3):
+                at = c * 8 + r % 7
+                result[c] = jnp.where(
+                    here, lane_pick(tab_ref[r // 7, at : at + 1, :], lanes_here), result[c]
+                )
+        results.append(result)
+    return [jnp.concatenate([result[c] for result in results], axis=0) for c in range(3)]
 
 
 def basis(dist_row, scaled_centers, gamma):
     diff = (-2.0 * gamma) * dist_row - scaled_centers
-    bump = jnp.exp2(diff * diff * (-math.log2(math.e) / (4.0 * gamma)))
+    bump = jnp.exp(diff * diff * (-1.0 / (4.0 * gamma)))
     return bump.astype(BF16), (diff * bump).astype(BF16)
 
 
@@ -207,43 +211,52 @@
         pl.semaphore_signal(barrier, inc=1, device_id=device, device_id_type=MESH)
 
     places[1] = jnp.zeros((PAD, LANES), F32)
-    wanted[...] = jnp.zeros_like(wanted)
     for c in range(3):
         for n in range(tiles):
             at = slice(n * LANES, (n + 1) * LANES)
             places[1, 8 * c + n : 8 * c + n + 1, :] = place_ref[c, :, at]
-            wanted[8 * c + n : 8 * c + n + 1, :] = wanted_ref[c, :, at]
+    pl.semaphore_wait(barrier, len(peers) + len(others))
+    targets = ((left, 2), (right, 0), (far, 3))
+    place_copies, state_copies = [], []
+    for i, (device, slot) in enumerate(targets):
+        place_copies.append(
+            send(places.at[1], places.at[slot], halo_send.at[i], halo_recv.at[i], {"graph": device})
+        )
     kind = (types_ref[...] == lax.broadcasted_iota(jnp.int32, (kinds, nodes), 0)).astype(BF16)
     embedded = lax.dot_general(
         table_ref[...], kind, (((0,), (0,)), ((), ())), preferred_element_type=F32
     )
     states[1] = (state_ref[...].astype(F32).T + embedded).astype(BF16)
-    prepare_indices(groups, source_ref, count_ref, lanes, rows_of, pick, compact, tiles)
-    pl.semaphore_wait(barrier, len(peers) + len(others))
-    place_copies, state_copies = [], []
-    targets = ((left, 2), (right, 0), (far, 3))
-    for i, (device, slot) in enumerate(targets):
-        place_copies.append(
-            send(places.at[1], places.at[slot], halo_send.at[i], halo_recv.at[i], {"graph": device})
-        )
-    for i, (device, slot) in enumerate(targets):
+
+    def send_state(i):
+        device, slot = targets[i]
         state_copies.append(
             send(
                 states.at[1], states.at[slot], halo_send.at[3 + i], halo_recv.at[3 + i], {"graph": device}
             )
         )
 
+    send_state(0)
+    send_state(1)
+
     w_rad_t[...] = w_rad_ref[...].astype(F32).T.astype(BF16)
     w_src_t[...] = w_src_ref[...].astype(F32).T.astype(BF16)
     w_out_t[...] = jnp.broadcast_to(w_out_ref[...], (channels, LANES)).T
+    wanted[...] = jnp.zeros_like(wanted)
+    for c in range(3):
+        for n in range(tiles):
+            at = slice(n * LANES, (n + 1) * LANES)
+            wanted[8 * c + n : 8 * c + n + 1, :] = wanted_ref[c, :, at]
     centre[...] = centers(count)[0]
     spread[...] = jnp.zeros_like(spread)
     incoming[...] = jnp.zeros_like(incoming)
     grad_radial[...] = jnp.zeros_like(grad_radial)
     grad_source[...] = jnp.zeros_like(grad_source)
     grad_out[...] = jnp.zeros_like(grad_out)
+    prepare_indices(groups, source_ref, count_ref, lanes, rows_of, pick, compact, tiles)
     for copy in place_copies:
         copy.wait()
+    send_state(2)
 
     def distances(n, table_rows):
         source_place = pick_three(places, table_rows, lanes[n], rows_of[n])
@@ -270,13 +283,14 @@
 
     lax.fori_loop(1, tiles, lambda n, u: (distances(n, 21), u)[1], 0)
     distances(0, 28)
-    def ahead(i, u):
+
+    def ahead(i, unused):
         bases(2 * i + 1, basis_a.at[i])
         bases(2 * i + 2, basis_b.at[i])
-        return u
+        return unused
 
     lax.fori_loop(0, tiles // 2, ahead, 0)
-    bases(0, basis_a.at[3])
+    bases(0, basis_a.at[tiles // 2])
     stack[10 * channels : 11 * channels, LANES:] = jnp.zeros((channels, LANES), BF16)
     for copy in state_copies[:2]:
         copy.wait()
@@ -462,25 +476,37 @@
     coefficients(0, 28, *coef_a)
     products(0, basis_a.at[tiles // 2], *coef_a)
 
+    def parts_of(value, number):
+        parts = []
+        for _ in range(number):
+            part = value.astype(BF16).astype(F32)
+            parts.append(part)
+            value = value - part
+        return parts
+
+    def piece_of(rows, out, loss):
+        more = parts_of(out, 2) + parts_of(loss, 3) + [jnp.zeros((3, LANES), F32)]
+        return jnp.concatenate([rows] + more, axis=0)
+
     radial = grad_radial[...].T
     source = grad_source[...]
+    nothing = jnp.zeros((1, LANES), F32)
     for i in range(groups):
-        for k in range(3):
-            at = (3 * i + k) * 8
-            own[i, 8 * k : 8 * k + 8] = (
-                radial[at : at + 8] if at < count else source[at - count : at - count + 8]
-            )
-        own[i, 24:] = jnp.zeros((8, LANES), F32)
-    own[0, 24:25] = jnp.sum(grad_out[...].T, axis=0, keepdims=True)
-    own[0, 25:26] = jnp.broadcast_to(loss, (1, LANES))
+        rows = [
+            radial[at : at + 8] if at < count else source[at - count : at - count + 8]
+            for at in range(24 * i, 24 * i + 24, 8)
+        ]
+        out = nothing if i else jnp.sum(grad_out[...].T, axis=0, keepdims=True)
+        total = nothing if i else jnp.broadcast_to(loss, (1, LANES))
+        own[i] = piece_of(jnp.concatenate(rows, axis=0), out, total).astype(BF16)
     copies = []
     for i, p in enumerate(peers):
         copies.append(send(own.at[p], pieces.at[i], piece_send.at[i], piece_recv.at[i], {"graph": p}))
     for copy in copies:
         copy.wait()
-    total = own[me]
+    total = own[me].astype(F32)
     for i in range(groups - 1):
-        total = total + pieces[i]
+        total = total + pieces[i].astype(F32)
     part[batch] = total
     copies = []
     for i, b in enumerate(others):
@@ -490,7 +516,9 @@
     total = part[0]
     for i in range(1, batches):
         total = total + part[i]
-    whole[me] = total
+    whole[me] = piece_of(
+        total[:24], total[24:25] + total[25:26], total[26:27] + total[27:28] + total[28:29]
+    ).astype(BF16)
     copies = []
     for i, p in enumerate(peers):
         copies.append(send(whole.at[me], whole.at[me], whole_send.at[i], whole_recv.at[i], {"graph": p}))
@@ -502,14 +530,16 @@
 def output_kernel(whole_ref, from_ref, forces_ref, radial_ref, source_ref, out_ref, loss_ref):
     count = radial_ref.shape[0]
     for i in range(whole_ref.shape[0]):
+        piece = whole_ref[i].astype(F32)
         for k in range(3):
             at = (3 * i + k) * 8
             if at < count:
-                radial_ref[at : at + 8] = whole_ref[i, 8 * k : 8 * k + 8]
+                radial_ref[at : at + 8] = piece[8 * k : 8 * k + 8]
             else:
-                source_ref[at - count : at - count + 8] = whole_ref[i, 8 * k : 8 * k + 8]
-    out_ref[...] = whole_ref[0, 24:25]
-    loss_ref[...] = whole_ref[0, 25:26, :1]
+                source_ref[at - count : at - count + 8] = piece[8 * k : 8 * k + 8]
+        if i == 0:
+            out_ref[...] = piece[24:25] + piece[25:26]
+            loss_ref[...] = (piece[26:27] + piece[27:28] + piece[28:29])[:, :1]
     forces_ref[...] = from_ref[...]
 
 
@@ -544,7 +574,7 @@
     others = max(batches - 1, 1)
     forces, whole = pl.pallas_call(
         functools.partial(fused_kernel, groups, batches, weight_loss),
-        out_shape=(shape(3, 1, nodes), shape(groups, 32, LANES)),
+        out_shape=(shape(3, 1, nodes), shape(groups, 32, LANES, dtype=BF16)),
         in_specs=[whole_vmem()] * 10,
         out_specs=(whole_vmem(),) * 2,
         scratch_shapes=[
@@ -579,10 +609,10 @@
             VMEM((channels, count), F32),
             VMEM((channels, channels), F32),
             VMEM((channels, LANES), F32),
-            VMEM((groups, 32, LANES), F32),
-            VMEM((groups - 1, 32, LANES), F32),
+            VMEM((groups, 32, LANES), BF16),
+            VMEM((groups - 1, 32, LANES), BF16),
             VMEM((batches, 32, LANES), F32),
-            VMEM((groups, 32, LANES), F32),
+            VMEM((groups, 32, LANES), BF16),
             dma((6,)),
             dma((6,)),
             dma((6,)),

time: 78.4 us -> 76 us (0.969)
  Pallas kernels: 76.9 us -> 74.6 us
    pallas_call x1, Pallas kernels: 75.3 us -> 73 us  [local(): pl.pallas_call(functools.partial(fused_kernel, groups, batches, weight_lo...]
where the time goes in v5:
time: 76 us; the launch traced here: 75.8 us
  Pallas kernels  74.6 us (98%)
  between operations  1.29 us (2%)
    pallas_call x1, Pallas kernels, local(): pl.pallas_call(functools.partial(fused_kernel, groups, batches, weight_lo...  73 us
    pallas_call x1, Pallas kernels, local(): pl.pallas_call(output_kernel, out_shape=(shape(3, 1, nodes), shape(count,...  1.6 us

profile of v5, /device:TPU:1, one launch (start us, length us, event | category | flops | bytes accessed | tf_op | source)
XLA Modules:
  0.0 75.8 jit_solution(16244227606585745367)
XLA Ops:
  1.3 73.0 %fused.1 = (f32[3,1,896]{2,1,0:T(1,128)}, bf16[16,32,128]{2,1,0:T(8,128)(2,1)}) custom-call(bf16[896,128]{1,0:T(8,128)(2,1)} %bitcast.7, s32[1,896]{1,0:T(1,128)} %types_ref.1, f32[3,1,896]{2,1,0:T(1,128)} %bitcast.8, f32[3,1,896]{2,1,0:T(1,128)} %bitcast.9, s32[1,17920]{1,0:T(1,128)} %source_ref.1, s32[1,1]{1,0:T(1,128)S(6)} %copy.15.count_ref, ...), custom_call_target="tpu_custom_call" | custom-call | tf_op jit(solution)/shard_map/fused/pallas_call | solution.py:575
  74.2 1.6 %output.1 = (f32[3,1,896]{2,1,0:T(1,128)}, f32[256,128]{1,0:T(8,128)}, f32[128,128]{1,0:T(8,128)}, f32[1,128]{1,0:T(1,128)}, f32[1,1]{1,0:T(1,128)}) custom-call(bf16[16,32,128]{2,1,0:T(8,128)(2,1)} %get-tuple-element.12.whole_ref, f32[3,1,896]{2,1,0:T(1,128)} %get-tuple-element.13.from_ref), custom_call_target="tpu_custom_call" | custom-call | tf_op jit(solution)/shard_map/output/pallas_call | solution.py:643

commit v6 on v5

--- a/solution.py
+++ b/solution.py
@@ -29,11 +29,12 @@
     return left, right, far
 
 
-def greet(devices):
-    barrier = pltpu.get_barrier_semaphore()
-    for device in devices:
-        pl.semaphore_signal(barrier, inc=1, device_id=device, device_id_type=MESH)
-    pl.semaphore_wait(barrier, len(devices))
+def farthest_first(count):
+    if count == 16:
+        return [4, 12, 5, 11, 3, 13, 6, 10, 2, 14, 7, 9, 8, 1, 15]
+    if count == 8:
+        return [3, 5, 4, 1, 7, 2, 6]
+    return list(range(1, count))
 
 
 def send(src, dst, send_sem, recv_sem, device):
@@ -203,8 +204,8 @@
     batch = lax.axis_index("dp")
     left, right, far = partners(groups)
     near_by = (left, right, far)
-    peers = [lax.rem(me + d, groups) for d in range(1, groups)]
-    others = [lax.rem(batch + d, batches) for d in range(1, batches)]
+    peers = [lax.rem(me + d, groups) for d in farthest_first(groups)]
+    others = [lax.rem(batch + d, batches) for d in farthest_first(batches)]
 
     barrier = pltpu.get_barrier_semaphore()
     for device in [{"graph": p} for p in peers] + [{"dp": b} for b in others]:
@@ -371,19 +372,18 @@
         for c in range(3):
             incoming[pl.ds(8 * c + n, 1), :] = inward[c]
 
-    agg_keep[0] = jnp.zeros((channels, LANES), F32)
-    product_b[...] = jnp.zeros_like(product_b)
-    onehots_b[...] = jnp.zeros_like(onehots_b)
-
     def two_forward(i, unused):
         n = 2 * i + 1
-        pull(n - 1, onehots_b, product_b)
-        gather(n, basis_a.at[i], onehots_a, product_a)
         pull(n, onehots_a, product_a)
         gather(n + 1, basis_b.at[i], onehots_b, product_b)
+        pull(n + 1, onehots_b, product_b)
+        gather(n + 2, basis_a.at[i + 1], onehots_a, product_a)
         return unused
 
-    lax.fori_loop(0, (tiles - 1) // 2, two_forward, 0)
+    gather(jnp.int32(1), basis_a.at[0], onehots_a, product_a)
+    lax.fori_loop(0, (tiles - 3) // 2, two_forward, 0)
+    pull(tiles - 2, onehots_a, product_a)
+    gather(jnp.int32(tiles - 1), basis_b.at[tiles // 2 - 1], onehots_b, product_b)
     state_copies[2].wait()
     stack_up(range(21, 28))
     pull(tiles - 1, onehots_b, product_b)
@@ -452,26 +452,26 @@
 
     def products(n, kept, plain_coef, slope_coef, wants):
         grad_radial[...] += lax.dot_general(
-            plain_coef[...], kept[0], NT, preferred_element_type=F32
-        ) + lax.dot_general(slope_coef[...], kept[1], NT, preferred_element_type=F32)
+            kept[0], plain_coef[...], NT, preferred_element_type=F32
+        ) + lax.dot_general(kept[1], slope_coef[...], NT, preferred_element_type=F32)
         grad_source[...] += lax.dot_general(
             rows_keep[n], wants[...], NT, preferred_element_type=F32
         )
 
     coef_a = (onehots_a.at[:channels], onehots_a.at[channels : 2 * channels], wants_a)
     coef_b = (onehots_b.at[:channels], onehots_b.at[channels : 2 * channels], wants_b)
-    for ref in coef_b:
-        ref[...] = jnp.zeros_like(ref)
-
     def two_backward(i, unused):
         n = 2 * i + 1
-        products(n - 1, basis_b.at[lax.max(i - 1, 0)], *coef_b)
-        coefficients(n, 21, *coef_a)
         products(n, basis_a.at[i], *coef_a)
         coefficients(n + 1, 21, *coef_b)
+        products(n + 1, basis_b.at[i], *coef_b)
+        coefficients(n + 2, 21, *coef_a)
         return unused
 
-    lax.fori_loop(0, (tiles - 1) // 2, two_backward, 0)
+    coefficients(1, 21, *coef_a)
+    lax.fori_loop(0, (tiles - 3) // 2, two_backward, 0)
+    products(tiles - 2, basis_a.at[tiles // 2 - 1], *coef_a)
+    coefficients(tiles - 1, 21, *coef_b)
     products(tiles - 1, basis_b.at[tiles // 2 - 1], *coef_b)
     coefficients(0, 28, *coef_a)
     products(0, basis_a.at[tiles // 2], *coef_a)
@@ -488,7 +488,7 @@
         more = parts_of(out, 2) + parts_of(loss, 3) + [jnp.zeros((3, LANES), F32)]
         return jnp.concatenate([rows] + more, axis=0)
 
-    radial = grad_radial[...].T
+    radial = grad_radial[...]
     source = grad_source[...]
     nothing = jnp.zeros((1, LANES), F32)
     for i in range(groups):
@@ -606,7 +606,7 @@
             VMEM((PAD, LANES), F32),
             VMEM((4, PAD, LANES), F32),
             *[VMEM((channels, wide), BF16)] * 2,
-            VMEM((channels, count), F32),
+            VMEM((count, channels), F32),
             VMEM((channels, channels), F32),
             VMEM((channels, LANES), F32),
             VMEM((groups, 32, LANES), BF16),

time: 76 us -> 75 us (0.987)
  Pallas kernels: 74.6 us -> 73.6 us
    pallas_call x1, Pallas kernels: 73 us -> 72 us  [local(): pl.pallas_call(functools.partial(fused_kernel, groups, batches, weight_lo...]
where the time goes in v6:
time: 75 us; the launch traced here: 74.8 us
  Pallas kernels  73.6 us (98%)
  between operations  1.29 us (2%)
    pallas_call x1, Pallas kernels, local(): pl.pallas_call(functools.partial(fused_kernel, groups, batches, weight_lo...  72 us
    pallas_call x1, Pallas kernels, local(): pl.pallas_call(output_kernel, out_shape=(shape(3, 1, nodes), shape(count,...  1.6 us

profile of v6, /device:TPU:1, one launch (start us, length us, event | category | flops | bytes accessed | tf_op | source)
XLA Modules:
  0.0 74.8 jit_solution(9783257527264720547)
XLA Ops:
  1.3 72.0 %fused.1 = (f32[3,1,896]{2,1,0:T(1,128)}, bf16[16,32,128]{2,1,0:T(8,128)(2,1)}) custom-call(bf16[896,128]{1,0:T(8,128)(2,1)} %bitcast.7, s32[1,896]{1,0:T(1,128)} %types_ref.1, f32[3,1,896]{2,1,0:T(1,128)} %bitcast.8, f32[3,1,896]{2,1,0:T(1,128)} %bitcast.9, s32[1,17920]{1,0:T(1,128)} %source_ref.1, s32[1,1]{1,0:T(1,128)S(6)} %copy.15.count_ref, ...), custom_call_target="tpu_custom_call" | custom-call | tf_op jit(solution)/shard_map/fused/pallas_call | solution.py:575
  73.2 1.6 %output.1 = (f32[3,1,896]{2,1,0:T(1,128)}, f32[256,128]{1,0:T(8,128)}, f32[128,128]{1,0:T(8,128)}, f32[1,128]{1,0:T(1,128)}, f32[1,1]{1,0:T(1,128)}) custom-call(bf16[16,32,128]{2,1,0:T(8,128)(2,1)} %get-tuple-element.12.whole_ref, f32[3,1,896]{2,1,0:T(1,128)} %get-tuple-element.13.from_ref), custom_call_target="tpu_custom_call" | custom-call | tf_op jit(solution)/shard_map/output/pallas_call | solution.py:643

commit v7 on v6

--- a/solution.py
+++ b/solution.py
@@ -282,7 +282,12 @@
                 (half % 2) * LANES : (half % 2 + 1) * LANES,
             ] = states[half // 7, :, at : at + LANES]
 
-    lax.fori_loop(1, tiles, lambda n, u: (distances(n, 21), u)[1], 0)
+    def three_distances(i, unused):
+        for k in range(1, 4):
+            distances(3 * i + k, 21)
+        return unused
+
+    lax.fori_loop(0, (tiles - 1) // 3, three_distances, 0)
     distances(0, 28)
 
     def ahead(i, unused):

time: 75 us -> 74.6 us (level)
  no operation moved by 1% of the time
where the time goes in v7:
time: 74.6 us; the launch traced here: 74.5 us
  Pallas kernels  73.2 us (98%)
  between operations  1.29 us (2%)
    pallas_call x1, Pallas kernels, local(): pl.pallas_call(functools.partial(fused_kernel, groups, batches, weight_lo...  71.6 us
    pallas_call x1, Pallas kernels, local(): pl.pallas_call(output_kernel, out_shape=(shape(3, 1, nodes), shape(count,...  1.6 us

profile of v7, /device:TPU:1, one launch (start us, length us, event | category | flops | bytes accessed | tf_op | source)
XLA Modules:
  0.0 74.5 jit_solution(10809998924172720130)
XLA Ops:
  1.3 71.6 %fused.1 = (f32[3,1,896]{2,1,0:T(1,128)}, bf16[16,32,128]{2,1,0:T(8,128)(2,1)}) custom-call(bf16[896,128]{1,0:T(8,128)(2,1)} %bitcast.7, s32[1,896]{1,0:T(1,128)} %types_ref.1, f32[3,1,896]{2,1,0:T(1,128)} %bitcast.8, f32[3,1,896]{2,1,0:T(1,128)} %bitcast.9, s32[1,17920]{1,0:T(1,128)} %source_ref.1, s32[1,1]{1,0:T(1,128)S(6)} %copy.15.count_ref, ...), custom_call_target="tpu_custom_call" | custom-call | tf_op jit(solution)/shard_map/fused/pallas_call | solution.py:580
  72.9 1.6 %output.1 = (f32[3,1,896]{2,1,0:T(1,128)}, f32[256,128]{1,0:T(8,128)}, f32[128,128]{1,0:T(8,128)}, f32[1,128]{1,0:T(1,128)}, f32[1,1]{1,0:T(1,128)}) custom-call(bf16[16,32,128]{2,1,0:T(8,128)(2,1)} %get-tuple-element.12.whole_ref, f32[3,1,896]{2,1,0:T(1,128)} %get-tuple-element.13.from_ref), custom_call_target="tpu_custom_call" | custom-call | tf_op jit(solution)/shard_map/output/pallas_call | solution.py:648
